TPU v7x, 32 devices: a whole 2x2x4 slice. The times are simulated.
32 devices in a mesh: grp: 2 (over x), lat: 16 (over z, y, core).
Axes of the slice: x: 2, y: 2, z: 4, core: 2. Of those that a mesh axis runs over, the one named last changes fastest.
Arguments:
- fields: bfloat16 [2, 32, 128, 384], P('grp', 'lat'), may hold values from -6 to 6
- cotangent: bfloat16 [2, 32, 128, 384], P('grp', 'lat'), may hold values from -6 to 6
- ocean_kernels: bfloat16 [2, 3, 3, 192, 192], replicated, may hold values from -0.15625 to 0.15625
- atmos_kernels: bfloat16 [2, 3, 3, 384, 384], replicated, may hold values from -0.109375 to 0.109375
- ocean_surface: bfloat16 [192, 4], replicated, may hold values from -0.4375 to 0.4375
- ocean_coupling: bfloat16 [4, 192], replicated, may hold values from -3 to 3
- atmos_flux: bfloat16 [384, 4], replicated, may hold values from -0.3125 to 0.3125
- atmos_coupling: bfloat16 [4, 384], replicated, may hold values from -3 to 3
- row_map: int32 [32], P('lat'), may hold values from 0 to 31, as said below
- wet_mask: int32 [32, 256], P('lat'), may hold values 0 or 1
Outputs:
- next_fields: bfloat16 [2, 32, 128, 384], P('grp', 'lat')
- field_grads: bfloat16 [2, 32, 128, 384], P('grp', 'lat')
- ocean_kernel_grad: float32 [663552], P(('grp', 'lat'))
- atmos_kernel_grad: float32 [2654208], P(('grp', 'lat'))
Inputs may be any that keep to these rules, and one draw needn't show every extreme that they name: row_map never falls, keeps each ocean row in its own band of 2 rows, and maps the first and last row of every band to that band's first and last row.
All inputs are finite; a program needn't handle non-finite values. No bound on the sum of `wet_mask` on one device may be relied on, other than what follows from the above.
Results may differ from a plain program's by a relative error of at most 0.0065.
Values may be sent and summed in bfloat16 or wider, within the bound.
No kernel may reach another device: no remote copies, remote signals or barrier semaphores. Data moves between devices by JAX's collectives and lax.ppermute only.
A program may use at most 128 MiB of HBM per device.

v0:
```python
import functools
import math

import jax
import jax.numpy as jnp
from jax import lax
from jax.experimental import pallas as pl
from jax.experimental.pallas import tpu as pltpu
from jax.sharding import PartitionSpec as P

HIGHEST = lax.Precision.HIGHEST
GELU_SCALE = 0.7978845608028654
GELU_CUBIC = 0.044715
F32 = jnp.float32
BF16 = jnp.bfloat16
WHOLE = pl.BlockSpec(memory_space=pltpu.VMEM)
IN_PLACE = pl.BlockSpec(memory_space=pl.ANY)
VMEM_LIMIT = 50 * 1024 * 1024

NN = (((1,), (0,)), ((), ()))
NT = (((1,), (1,)), ((), ()))
TN = (((0,), (0,)), ((), ()))


def shape(dims, kind):
    return jax.ShapeDtypeStruct(dims, kind)


def call(kernel, outs, inputs, in_specs=None, scratch=(), flops=0, moved=0, name=None):
    return pl.pallas_call(
        kernel,
        out_shape=outs,
        in_specs=in_specs or [WHOLE] * len(inputs),
        out_specs=jax.tree.map(lambda _: WHOLE, outs),
        scratch_shapes=list(scratch),
        compiler_params=pltpu.CompilerParams(vmem_limit_bytes=VMEM_LIMIT),
        cost_estimate=pl.CostEstimate(flops=flops, bytes_accessed=moved, transcendentals=0),
        name=name,
    )(*inputs)


def on_ocean():
    return lax.axis_index("grp") == 0


def dot(left, right, dims=NN, precision=None):
    return lax.dot_general(left, right, dims, precision=precision, preferred_element_type=F32)


def moved_cells(values, axis, cols):
    count = values.shape[axis]
    place = lax.rem(lax.broadcasted_iota(jnp.int32, values.shape, axis), cols)
    before = jnp.where(place == 0, 0.0, pltpu.roll(values, 1, axis))
    after = jnp.where(place == cols - 1, 0.0, pltpu.roll(values, count - 1, axis))
    return before, after


def pack_kernel(x_ref, g_ref, wet_ref, up_ref, down_ref, own_ref, *, cols):
    wet = wet_ref[...].astype(F32)
    source = lax.broadcasted_iota(jnp.int32, (2 * cols, 2 * cols), 0)
    target = lax.broadcasted_iota(jnp.int32, (2 * cols, 2 * cols), 1)
    wanted = 2 * lax.rem(target, cols) + jnp.where(target >= cols, 1, 0)
    chooser = (source == wanted).astype(F32).astype(BF16)
    padded = jnp.concatenate([wet, jnp.zeros((14, 2 * cols), F32)], axis=0)
    apart = dot(padded.astype(BF16), chooser)
    wide = jnp.concatenate([apart, jnp.zeros((16, x_ref.shape[2] - 2 * cols), F32)], axis=1)
    own_ref[...] = wide.astype(BF16)
    other = pltpu.roll(wide, 15, 0)
    up_ref[0:cols, :] = x_ref[1]
    up_ref[cols : 2 * cols, :] = g_ref[1]
    up_ref[2 * cols :, :] = other.astype(BF16)
    down_ref[0:cols, :] = x_ref[0]
    down_ref[cols : 2 * cols, :] = g_ref[0]
    down_ref[2 * cols :, :] = wide.astype(BF16)


def expand_kernel(raw_ref, out_ref):
    narrow = raw_ref.shape[2]

    @pl.when(on_ocean())
    def _():
        row = lax.broadcasted_iota(jnp.int32, (narrow, 2 * narrow), 0)
        col = lax.broadcasted_iota(jnp.int32, (narrow, 2 * narrow), 1)
        to_left = (row == col).astype(F32).astype(BF16)
        to_right = (row + narrow == col).astype(F32).astype(BF16)
        nothing = jnp.zeros((narrow, 2 * narrow), BF16)

        def step(index, carry):
            first, middle, last = (raw_ref[3 * index + tap] for tap in range(3))
            out_ref[3 * index, 0:narrow, :] = nothing
            out_ref[3 * index, narrow:, :] = dot(first, to_left).astype(BF16)
            even = dot(middle, to_left) + dot(first, to_right)
            odd = dot(last, to_left) + dot(middle, to_right)
            out_ref[3 * index + 1, 0:narrow, :] = even.astype(BF16)
            out_ref[3 * index + 1, narrow:, :] = odd.astype(BF16)
            out_ref[3 * index + 2, 0:narrow, :] = dot(last, to_right).astype(BF16)
            out_ref[3 * index + 2, narrow:, :] = nothing
            return carry

        lax.fori_loop(0, raw_ref.shape[0] // 3, step, 0)


def outgoing_kernel(
    x_ref, g_ref, low_ref, high_ref, own_ref, terms_ref,
    xpad_ref, gpad_ref, wet_ref, early_ref, sent_ref, *, cols,
):
    for pad_ref, own, start in ((xpad_ref, x_ref, 0), (gpad_ref, g_ref, cols)):
        pad_ref[0:cols, :] = low_ref[start : start + cols, :]
        pad_ref[cols : 2 * cols, :] = own[0]
        pad_ref[2 * cols : 3 * cols, :] = own[1]
        pad_ref[3 * cols : 4 * cols, :] = high_ref[start : start + cols, :]
    low_wet = low_ref[2 * cols :, :].astype(F32)
    high_wet = high_ref[2 * cols :, :].astype(F32)
    own_wet = own_ref[...].astype(F32)
    halves = []
    for start in (0, cols):
        lanes = slice(start, start + cols)
        rows = (low_wet[0:1, lanes], own_wet[0:1, lanes], own_wet[1:2, lanes], high_wet[0:1, lanes])
        halves.append(jnp.concatenate(rows, axis=1))
    first_wet, second_wet = halves
    inverse = 1.0 / jnp.maximum(first_wet + second_wet, 1.0)
    wet_ref[0:1, :] = first_wet
    wet_ref[1:2, :] = second_wet
    wet_ref[2:3, :] = inverse
    wet_ref[3:8, :] = jnp.zeros((5, 4 * cols), F32)
    xpad = xpad_ref[...]
    projected = dot(terms_ref[0:8, :].astype(BF16), xpad, NT)
    mixed = (projected[0:4] * first_wet + projected[4:8] * second_wet) * inverse
    sent_ref[...] = jnp.where(on_ocean(), mixed, projected[0:4])
    early_ref[...] = jnp.where(on_ocean(), gpad_ref[...], xpad)


def fetch(atmos_ref, ocean_ref, where, buffer, sem):
    @pl.when(on_ocean())
    def _():
        pltpu.make_async_copy(ocean_ref.at[where], buffer, sem).start()

    @pl.when(jnp.logical_not(on_ocean()))
    def _():
        pltpu.make_async_copy(atmos_ref.at[where], buffer, sem).start()

    return pltpu.make_async_copy(atmos_ref.at[where], buffer, sem)


def with_columns(pad, cols):
    before, after = moved_cells(pad.astype(F32), 0, cols)
    return before.astype(BF16), pad, after.astype(BF16)


def conv(pad, weight_ref, base, cols):
    taps = with_columns(pad, cols)
    joined = jnp.concatenate(taps, axis=1)
    rows = pad.shape[0] - 2 * cols
    channels = pad.shape[1]
    total = None
    for tap in range(3):
        kernel = weight_ref[base + 3 * tap : base + 3 * tap + 3].reshape(3 * channels, channels)
        part = dot(joined[cols * tap : cols * tap + rows], kernel)
        total = part if total is None else total + part
    return total


def conv_back(pad, weight_ref, base, cols):
    taps = with_columns(pad, cols)
    rows = pad.shape[0] - 2 * cols
    total = None
    for row_tap in range(3):
        for col_tap in range(3):
            kernel = weight_ref[base + 8 - (3 * row_tap + col_tap)]
            part = dot(taps[col_tap][cols * row_tap : cols * row_tap + rows], kernel, NT)
            total = part if total is None else total + part
    return total


def back_kernel(gpad_ref, atmos_ref, ocean_ref, out_ref, buffer, sem, *, cols):
    copy = fetch(atmos_ref, ocean_ref, pl.ds(9, 9), buffer, sem)
    copy.wait()
    out_ref[...] = conv_back(gpad_ref[...], buffer, 0, cols)


def spread(arrived, wet, mixing, terms):
    first_wet, second_wet = wet
    both = jnp.concatenate([arrived * first_wet, arrived * second_wet], axis=0)
    alone = jnp.concatenate([arrived, jnp.zeros_like(arrived)], axis=0)
    return dot(jnp.where(mixing, both, alone), terms, TN, HIGHEST)


def first_kernel(
    xpad_ref, wet_ref, arrived_ref, terms_ref, back_ref, atmos_ref, ocean_ref,
    u_ref, stay_ref, give_ref, up_ref, down_ref, buffer, sem, *, cols,
):
    copy = fetch(atmos_ref, ocean_ref, pl.ds(0, 9), buffer, sem)
    wet = wet_ref[0:1, :], wet_ref[1:2, :]
    coupled = spread(arrived_ref[...], wet, on_ocean(), terms_ref[8:16, :])
    u = (xpad_ref[...].astype(F32) + coupled).astype(BF16)
    u_ref[...] = u
    copy.wait()
    first = conv(u, buffer, 0, cols)
    tangent = jnp.tanh(GELU_SCALE * (first + GELU_CUBIC * first * first * first))
    hidden = (0.5 * first * (1.0 + tangent)).astype(BF16)
    slope = 0.5 * (1.0 + tangent) + 0.5 * first * (1.0 - tangent * tangent) * GELU_SCALE * (
        1.0 + 3.0 * GELU_CUBIC * first * first
    )
    first_grad = (back_ref[...] * slope).astype(BF16)
    stay_ref[...] = jnp.where(on_ocean(), first_grad, hidden)
    give_ref[...] = jnp.where(on_ocean(), hidden, first_grad)
    up_ref[0:cols, :] = hidden[cols:]
    up_ref[cols:, :] = first_grad[cols:]
    down_ref[0:cols, :] = hidden[:cols]
    down_ref[cols:, :] = first_grad[:cols]


def grad_atmos(pad, own, pad_is_input, cols, store):
    rows = own.shape[0]
    if pad_is_input:
        middle = pad.T
        before, after = moved_cells(middle, 1, cols)
        lefts = [part.astype(BF16) for part in (before, middle, after)]
        right = own.astype(BF16)
        for tap in range(9):
            start = cols * (tap // 3)
            store(tap, dot(lefts[tap % 3][:, start : start + rows], right))
    else:
        left = own.T.astype(BF16)
        before, after = moved_cells(pad, 0, cols)
        rights = [part.astype(BF16) for part in (after, pad, before)]
        for tap in range(9):
            start = cols * (2 - tap // 3)
            store(tap, dot(left, rights[tap % 3][start : start + rows]))


def grad_ocean(pad, own, pad_is_input, cols, store):
    rows, channels = own.shape
    narrow = channels // 2
    wide = -(-narrow // 128) * 128

    def apart(values):
        lane = lax.broadcasted_iota(jnp.int32, values.shape, 1)
        even = jnp.where(lane < narrow, values, 0.0)
        odd = jnp.where(lane < narrow, pltpu.roll(values, narrow, 1), 0.0)
        return even[:, :wide], odd[:, :wide]

    if pad_is_input:
        middle = pad.T
        before, after = moved_cells(middle, 1, cols)
        even, odd = middle[:narrow].astype(BF16), middle[narrow:].astype(BF16)
        pairs = (
            (before[narrow:].astype(BF16), even),
            (even, odd),
            (odd, after[:narrow].astype(BF16)),
        )
        right = jnp.concatenate(apart(own), axis=0).astype(BF16)
        for tap in range(9):
            start = cols * (tap // 3)
            pieces = [part[:, start : start + rows] for part in pairs[tap % 3]]
            store(tap, dot(jnp.concatenate(pieces, axis=1), right))
    else:
        turned = own.T.astype(BF16)
        left = jnp.concatenate([turned[:narrow], turned[narrow:]], axis=1)
        even, odd = apart(pad)
        odd_before = moved_cells(odd, 0, cols)[0].astype(BF16)
        even_after = moved_cells(even, 0, cols)[1].astype(BF16)
        even, odd = even.astype(BF16), odd.astype(BF16)
        pairs = ((odd, even_after), (even, odd), (odd_before, even))
        for tap in range(9):
            start = cols * (2 - tap // 3)
            pieces = [part[start : start + rows] for part in pairs[tap % 3]]
            store(tap, dot(left, jnp.concatenate(pieces, axis=0)))


def both_grads(
    early_ref, upad_ref, gpad_ref, stay_ref, late_ref, sent_ref, coupling_ref, atmos_out, ocean_out, cols
):
    channels = upad_ref.shape[1]
    narrow = channels // 2

    def store_atmos(tap, value):
        atmos_out[channels * tap : channels * (tap + 1), :] = value

    def store_ocean(tap, value):
        for piece in range(ocean_out.shape[0]):
            lanes = slice(128 * piece, 128 * (piece + 1))
            ocean_out[piece, narrow * tap : narrow * (tap + 1), :] = value[:, lanes]

    @pl.when(on_ocean())
    def _():
        added = dot(sent_ref[...], coupling_ref[...].astype(F32), TN, HIGHEST)
        other = (early_ref[...].astype(F32) + added).astype(BF16).astype(F32)
        grad_ocean(upad_ref[...].astype(F32), stay_ref[...].astype(F32), True, cols, store_ocean)
        grad_atmos(other, late_ref[...].astype(F32), True, cols, store_atmos)

    @pl.when(jnp.logical_not(on_ocean()))
    def _():
        grad_atmos(gpad_ref[...].astype(F32), stay_ref[...].astype(F32), False, cols, store_atmos)
        grad_ocean(early_ref[...].astype(F32), late_ref[...].astype(F32), False, cols, store_ocean)


def grads_kernel(*refs, cols, chunks):
    ins, (keep_ref, send_ref, atmos_all, ocean_all) = refs[:7], refs[7:]
    both_grads(*ins, atmos_all, ocean_all, cols)
    channels = keep_ref.shape[2]
    pieces = ocean_all.shape[0]
    atmos_rows = atmos_all.shape[0] // chunks
    ocean_rows = atmos_rows // 2
    taken = keep_ref.shape[1] - atmos_rows
    spare = ocean_all.shape[1] - ocean_rows * chunks
    if spare:
        ocean_all[:, ocean_rows * chunks :, :] = jnp.zeros((pieces, spare, 128), F32)
    core = lax.rem(lax.axis_index("lat"), 2)
    blank = jnp.zeros((taken, channels - 128 * pieces), F32)
    for out_ref, side in ((send_ref, 1 - core), (keep_ref, core)):
        for pair in range(chunks // 2):
            start = pl.multiple_of(atmos_rows * (2 * pair + side), 8)
            upper = atmos_all[pl.ds(start, atmos_rows), :]
            start = ocean_rows * (2 * pair + side)
            halves = []
            for odd in range(2):
                parts = [ocean_all.at[piece][pl.ds(start + odd, taken, 2), :] for piece in range(pieces)]
                halves.append(jnp.concatenate(parts + [blank], axis=1))
            lower = halves[0] + pltpu.roll(halves[1], channels // 2, 1)
            out_ref[pair] = jnp.concatenate([upper, lower], axis=0).astype(BF16)


def own_bit(bit):
    return lax.rem(lax.shift_right_logical(lax.axis_index("lat"), bit), 2)


def halve(keep_ref, came_ref, keep_out, send_out, bit, rows):
    own = own_bit(bit)
    for out_ref, side in ((send_out, 1 - own), (keep_out, own)):
        for outer in range(keep_ref.shape[0]):
            for inner in range(keep_ref.shape[2]):
                total = keep_ref[outer, side, inner, rows, :].astype(F32)
                total = total + came_ref[outer, side, inner, rows, :].astype(F32)
                out_ref[outer, inner] = total.astype(BF16)


def split_kernel(keep_ref, came_ref, first_keep, first_send, second_keep, second_send, *, cut):
    tall = keep_ref.shape[3]
    halve(keep_ref, came_ref, first_keep, first_send, 1, slice(0, cut))
    views = [ref.reshape(2, 2, 2, *keep_ref.shape[3:]) for ref in (keep_ref, came_ref)]
    halve(*views, second_keep, second_send, 2, slice(cut, tall))


def halve_kernel(keep_ref, came_ref, keep_out, send_out, *, bit):
    halve(keep_ref, came_ref, keep_out, send_out, bit, slice(None))


def halved(keep, came, bit, dims):
    outer, inner, rows, channels = dims[0], dims[1], keep.shape[-2], keep.shape[-1]
    keep, came = (part.reshape(outer, 2, inner, rows, channels) for part in (keep, came))
    out = shape((outer, inner, rows, channels), BF16)
    return call(
        functools.partial(halve_kernel, bit=bit),
        [out, out],
        [keep, came],
        moved=8 * outer * inner * rows * channels,
        name="halve",
    )


def scatter_sum(keep, send):
    pairs, tall, channels = keep.shape
    came = swapped(send, "lat", 1)
    cut = -(-tall // 32) * 16
    first, second = shape((4, 1, cut, channels), BF16), shape((2, 2, tall - cut, channels), BF16)
    keep, came = (part.reshape(4, 2, 1, tall, channels) for part in (keep, came))
    first_keep, first_send, second_keep, second_send = call(
        functools.partial(split_kernel, cut=cut),
        [first, first, second, second],
        [keep, came],
        moved=6 * pairs * tall * channels,
        name="split",
    )
    first_came = swapped(first_send, "lat", 2)
    second_came = swapped(second_send, "lat", 4)
    first_keep, first_send = halved(first_keep, first_came, 2, (2, 1))
    first_came = swapped(first_send, "lat", 4)
    second_keep, second_send = halved(second_keep, second_came, 3, (1, 2))
    second_came = swapped(second_send, "lat", 8)
    first_keep, first_send = halved(first_keep, first_came, 3, (1, 1))
    first_came = swapped(first_send, "lat", 8)
    second_keep, second_send = halved(second_keep, second_came, 1, (1, 1))
    second_came = swapped(second_send, "lat", 2)
    return [part.reshape(-1, channels) for part in (first_keep, first_came, second_keep, second_came)]


def plain_grads_kernel(*refs, cols):
    both_grads(*refs, cols)


def finish_kernel(
    first_ref, first_came, second_ref, second_came, atmos_ref, ocean_ref, *, atmos_factor, ocean_factor
):
    channels = first_ref.shape[1]
    pieces = channels // 128
    atmos_rows = atmos_ref.shape[0] // pieces
    ocean_rows = ocean_ref.shape[0] // pieces
    first = first_ref[...].astype(F32) + first_came[...].astype(F32)
    second = second_ref[...].astype(F32) + second_came[...].astype(F32)
    total = jnp.concatenate([first, second], axis=0)
    for piece in range(pieces):
        lanes = slice(128 * piece, 128 * (piece + 1))
        atmos_ref[pl.ds(piece, atmos_rows, pieces), :] = total[:atmos_rows, lanes] * atmos_factor
        ocean_ref[pl.ds(piece, ocean_rows, pieces), :] = (
            total[atmos_rows : atmos_rows + ocean_rows, lanes] * ocean_factor
        )


def next_kernel(
    stay_ref, give_ref, low_ref, high_ref, upad_ref, gpad_ref, wet_ref, terms_ref, atmos_ref, ocean_ref,
    next_ref, grad_ref, sent_ref, buffer, sem, *, cols,
):
    copy = fetch(atmos_ref, ocean_ref, pl.ds(0, 18), buffer, sem)
    hidden = jnp.where(on_ocean(), give_ref[...], stay_ref[...])
    first_grad = jnp.where(on_ocean(), stay_ref[...], give_ref[...])
    hidden_pad = jnp.concatenate([low_ref[0:cols, :], hidden, high_ref[0:cols, :]], axis=0)
    first_pad = jnp.concatenate([low_ref[cols:, :], first_grad, high_ref[cols:, :]], axis=0)
    own = slice(cols, 3 * cols)
    copy.wait()
    grad = gpad_ref[own, :].astype(F32) + conv_back(first_pad, buffer, 0, cols)
    grad_ref[...] = grad
    weighted = dot(terms_ref[8:16, :], grad, NT, HIGHEST)
    mixed = weighted[0:4] * wet_ref[0:1, own] + weighted[4:8] * wet_ref[1:2, own]
    sent_ref[...] = jnp.where(on_ocean(), mixed, weighted[0:4])
    second = conv(hidden_pad, buffer, 9, cols)
    values = (upad_ref[own, :].astype(F32) + second).astype(BF16)
    next_ref[0] = values[:cols]
    next_ref[1] = values[cols:]


def last_kernel(grad_ref, arrived_ref, wet_ref, terms_ref, out_ref, *, cols):
    own = slice(cols, 3 * cols)
    wet = wet_ref[0:1, own], wet_ref[1:2, own]
    arrived = jnp.where(on_ocean(), arrived_ref[...] * wet_ref[2:3, own], arrived_ref[...])
    added = spread(arrived, wet, on_ocean(), terms_ref[0:8, :])
    values = (grad_ref[...] + added).astype(BF16)
    out_ref[0] = values[:cols]
    out_ref[1] = values[cols:]


def swapped(value, axis, mask):
    pairs = [(source, source ^ mask) for source in range(lax.axis_size(axis))]
    return lax.ppermute(value, axis, pairs)


def halo(up, down):
    count = lax.axis_size("lat")
    forward = [(i, i + 1) for i in range(count - 1)]
    backward = [(target, source) for source, target in forward]
    return lax.ppermute(up, "lat", forward), lax.ppermute(down, "lat", backward)


def local(
    fields,
    cotangent,
    ocean_kernels,
    atmos_kernels,
    ocean_surface,
    ocean_coupling,
    atmos_flux,
    atmos_coupling,
    row_map,
    wet_mask,
):
    x, g = fields[0], cotangent[0]
    bands, cols, channels = x.shape
    narrow = channels // 2
    cells = bands * cols
    count = lax.axis_size("lat")
    is_ocean = lax.axis_index("grp") == 0
    atmos_factor = 1.0 / math.sqrt(bands * count * cols)
    ocean_factor = 1.0 / math.sqrt(bands * count * 2 * cols)
    bound = functools.partial

    blank = jnp.zeros((4, narrow), BF16)
    gap = jnp.zeros((4, channels), BF16)
    surface = ocean_surface.T
    ocean_terms = jnp.concatenate(
        [
            jnp.concatenate([surface, blank], axis=1),
            jnp.concatenate([blank, surface], axis=1),
            jnp.concatenate([ocean_coupling, blank], axis=1),
            jnp.concatenate([blank, ocean_coupling], axis=1),
        ],
        axis=0,
    )
    atmos_terms = jnp.concatenate([atmos_flux.T, gap, atmos_coupling, gap], axis=0)
    terms = jnp.where(is_ocean, ocean_terms, atmos_terms).astype(F32)

    edge = shape((2 * cols + 16, channels), BF16)
    up, down, own_wet = call(
        bound(pack_kernel, cols=cols), [edge, edge, shape((16, channels), BF16)], [x, g, wet_mask], name="pack"
    )
    low, high = halo(up, down)
    atmos_flat = atmos_kernels.reshape(18, channels, channels)
    ocean_flat = call(
        expand_kernel,
        shape((18, channels, channels), BF16),
        [ocean_kernels.reshape(18, narrow, narrow)],
        flops=2 * 36 * narrow * narrow * channels,
        moved=18 * channels * channels * 2,
        name="expand",
    )
    pad = shape((2 * cells, channels), BF16)
    xpad, gpad, wet, early, sent = call(
        bound(outgoing_kernel, cols=cols),
        [pad, pad, shape((8, 2 * cells), F32), pad, shape((4, 2 * cells), F32)],
        [x, g, low, high, own_wet, terms],
        name="outgoing",
    )
    arrived = swapped(sent, "grp", 1)
    other_early = swapped(early, "grp", 1)
    one_conv = 2 * 9 * cells * channels * channels
    weight_bytes = 9 * channels * channels * 2
    buffer = [pltpu.VMEM((9, channels, channels), BF16), pltpu.SemaphoreType.DMA]
    back = call(
        bound(back_kernel, cols=cols),
        shape((cells, channels), F32),
        [gpad, atmos_flat, ocean_flat],
        [WHOLE, IN_PLACE, IN_PLACE],
        buffer,
        flops=one_conv,
        moved=weight_bytes,
        name="back",
    )
    half = shape((cells, channels), BF16)
    upad, stay, give, up, down = call(
        bound(first_kernel, cols=cols),
        [pad, half, half, half, half],
        [xpad, wet, arrived, terms, back, atmos_flat, ocean_flat],
        [WHOLE] * 5 + [IN_PLACE] * 2,
        buffer,
        flops=one_conv,
        moved=weight_bytes,
        name="first",
    )
    late = swapped(give, "grp", 1)

    atmos_rows = 9 * channels // count
    ocean_rows = 9 * narrow // count
    inputs = [other_early, upad, gpad, stay, late, sent, atmos_coupling]
    wide = -(-narrow // 128) * 128
    if count == 16 and 9 * channels % (8 * count) == 0 and ocean_rows % 2 == 0:
        tall = -(-(atmos_rows + ocean_rows // 2) // 16) * 16
        taken = tall - atmos_rows
        spare = max(0, 2 * taken - ocean_rows)
        part = shape((count // 2, tall, channels), BF16)
        keep, send = call(
            bound(grads_kernel, cols=cols, chunks=count),
            [part, part],
            inputs,
            None,
            [
                pltpu.VMEM((9 * channels, channels), F32),
                pltpu.VMEM((wide // 128, 9 * narrow + -(-spare // 8) * 8, 128), F32),
            ],
            flops=2 * one_conv,
            moved=count * tall * channels * 2,
            name="grads",
        )
        atmos_chunk, ocean_chunk = call(
            bound(finish_kernel, atmos_factor=atmos_factor, ocean_factor=ocean_factor),
            [
                shape((atmos_rows * channels // 128, 128), F32),
                shape((ocean_rows * narrow // 128, 128), F32),
            ],
            scatter_sum(keep, send),
            name="finish",
        )
        atmos_total, ocean_total = atmos_chunk.reshape(-1), ocean_chunk.reshape(-1)
    else:
        atmos_all, ocean_all = call(
            bound(plain_grads_kernel, cols=cols),
            [shape((9 * channels, channels), F32), shape((wide // 128, 9 * narrow, 128), F32)],
            inputs,
            flops=2 * one_conv,
            name="grads",
        )
        atmos_total = atmos_factor * lax.psum_scatter(
            atmos_all.reshape(-1), "lat", scatter_dimension=0, tiled=True
        )
        ocean_all = jnp.concatenate([ocean_all[piece] for piece in range(wide // 128)], axis=1)
        ocean_total = ocean_factor * lax.psum_scatter(
            ocean_all[:, :narrow].reshape(-1), "lat", scatter_dimension=0, tiled=True
        )

    low, high = halo(up, down)
    next_field, grad, sent_back = call(
        bound(next_kernel, cols=cols),
        [shape(x.shape, BF16), shape((cells, channels), F32), shape((4, cells), F32)],
        [stay, give, low, high, upad, gpad, wet, terms, atmos_flat, ocean_flat],
        [WHOLE] * 8 + [IN_PLACE] * 2,
        [pltpu.VMEM((18, channels, channels), BF16), pltpu.SemaphoreType.DMA],
        flops=2 * one_conv,
        moved=2 * weight_bytes,
        name="next",
    )
    returned = swapped(sent_back, "grp", 1)
    field_grad = call(
        bound(last_kernel, cols=cols), shape(x.shape, BF16), [grad, returned, wet, terms], name="last"
    )
    return (next_field[None], field_grad[None], ocean_total, atmos_total)


def solution(mesh):
    in_specs = (
        P("grp", "lat", None, None),
        P("grp", "lat", None, None),
        P(),
        P(),
        P(),
        P(),
        P(),
        P(),
        P("lat"),
        P("lat", None),
    )
    out_specs = (
        P("grp", "lat", None, None),
        P("grp", "lat", None, None),
        P(("grp", "lat")),
        P(("grp", "lat")),
    )
    return jax.shard_map(local, mesh=mesh, in_specs=in_specs, out_specs=out_specs, check_vma=False)
```

profile of v0, /device:TPU:0, one launch (start us, length us, event | category | flops | bytes accessed | tf_op | source)
XLA Modules:
  0.0 90.7 jit_solution(11641737681512373519)
XLA Ops:
  0.6 0.9 %copy-done.1 = bf16[1,2,128,384]{3,2,1,0:T(8,128)(2,1)S(1)} copy-done((bf16[1,2,128,384]{3,2,1,0:T(8,128)(2,1)S(1)}, bf16[1,2,128,384]{3,2,1,0:T(8,128)(2,1)}, u32[]{:S(2)}) %copy-start.1) | copy-done | bytes 196632
  1.6 0.9 %copy-done.3 = bf16[1,2,128,384]{3,2,1,0:T(8,128)(2,1)S(1)} copy-done((bf16[1,2,128,384]{3,2,1,0:T(8,128)(2,1)S(1)}, bf16[1,2,128,384]{3,2,1,0:T(8,128)(2,1)}, u32[]{:S(2)}) %copy-start.3) | copy-done | bytes 196632
  3.3 2.4 %collective-permute-start = (bf16[272,384]{1,0:T(8,128)(2,1)S(1)}, bf16[272,384]{1,0:T(8,128)(2,1)S(1)}, u32[]{:S(2)}, u32[]{:S(2)}) collective-permute-start(bf16[272,384]{1,0:T(8,128)(2,1)S(1)} %get-tuple-element.36), channel_id=1, source_target_pairs={{0,1},{1,2},{2,3},{3,4},{4,5},{5,6},{6,7},{7,8},{8,9},{9,10},{10,1... | collective-permute-start | bytes 626696 | tf_op jit(solution)/shard_map/ppermute | solution.py:451
  5.7 1.3 %collective-permute-start.1 = (bf16[272,384]{1,0:T(8,128)(2,1)S(1)}, bf16[272,384]{1,0:T(8,128)(2,1)S(1)}, u32[]{:S(2)}, u32[]{:S(2)}) collective-permute-start(bf16[272,384]{1,0:T(8,128)(2,1)S(1)} %get-tuple-element.37), channel_id=1, source_target_pairs={{1,0},{2,1},{3,2},{4,3},{5,4},{6,5},{7,6},{8,7},{9,8},{10,9},{11,1... | collective-permute-start | bytes 626696 | tf_op jit(solution)/shard_map/ppermute | solution.py:451
  7.9 3.3 %collective-permute-done.1.high_ref = bf16[272,384]{1,0:T(8,128)(2,1)S(1)} collective-permute-done((bf16[272,384]{1,0:T(8,128)(2,1)S(1)}, bf16[272,384]{1,0:T(8,128)(2,1)S(1)}, u32[]{:S(2)}, u32[]{:S(2)}) %collective-permute-start.1) | collective-permute-done | bytes 208928 | tf_op jit(solution)/shard_map/ppermute | solution.py:451
  11.2 0.9 %copy-done.2 = bf16[1,2,128,384]{3,2,1,0:T(8,128)(2,1)S(1)} copy-done((bf16[1,2,128,384]{3,2,1,0:T(8,128)(2,1)S(1)}, bf16[1,2,128,384]{3,2,1,0:T(8,128)(2,1)}, u32[]{:S(2)}) %copy-start.2) | copy-done | bytes 196632
  12.1 0.9 %copy-done.4 = bf16[1,2,128,384]{3,2,1,0:T(8,128)(2,1)S(1)} copy-done((bf16[1,2,128,384]{3,2,1,0:T(8,128)(2,1)S(1)}, bf16[1,2,128,384]{3,2,1,0:T(8,128)(2,1)}, u32[]{:S(2)}) %copy-start.4) | copy-done | bytes 196632
  13.3 1.5 %collective-permute-start.6 = (bf16[512,384]{1,0:T(8,128)(2,1)S(1)}, bf16[512,384]{1,0:T(8,128)(2,1)S(1)}, u32[]{:S(2)}, u32[]{:S(2)}) collective-permute-start(bf16[512,384]{1,0:T(8,128)(2,1)S(1)} %get-tuple-element.51), channel_id=1, source_target_pairs={{0,16},{16,0},{1,17},{17,1},{2,18},{18,2},{3,19},{19,3},{4,20},{20... | collective-permute-start | bytes 1179656 | tf_op jit(solution)/shard_map/ppermute | solution.py:444
  14.9 1.5 %copy-done = bf16[2,3,3,192,192]{4,3,2,1,0:T(8,128)(2,1)S(1)} copy-done((bf16[2,3,3,192,192]{4,3,2,1,0:T(8,128)(2,1)S(1)}, bf16[2,3,3,192,192]{4,3,2,1,0:T(8,128)(2,1)}, u32[]{:S(2)}) %copy-start) | copy-done | bytes 1327128
  16.3 5.2 %expand.1.ocean_ref = bf16[18,384,384]{2,1,0:T(8,128)(2,1)} custom-call(bf16[18,192,192]{2,1,0:T(8,128)(2,1)S(1)} %bitcast.25), custom_call_target="tpu_custom_call" | custom-call | flops 1019215872 | bytes 5308416 | tf_op jit(solution)/shard_map/expand/pallas_call | solution.py:30
  21.5 3.0 %back.1.back_ref = f32[256,384]{1,0:T(8,128)S(1)} custom-call(bf16[512,384]{1,0:T(8,128)(2,1)S(1)} %get-tuple-element.42.gpad_ref.refs_2_, bf16[18,384,384]{2,1,0:T(8,128)(2,1)} %bitcast.44, bf16[18,384,384]{2,1,0:T(8,128)(2,1)} %expand.1.ocean_ref), custom_call_target="tpu_custom_call" | custom-call | flops 679477248 | bytes 2654208 | tf_op jit(solution)/shard_map/back/pallas_call | solution.py:30
  25.3 3.4 %first.1 = (bf16[512,384]{1,0:T(8,128)(2,1)S(1)}, bf16[256,384]{1,0:T(8,128)(2,1)S(1)}, bf16[256,384]{1,0:T(8,128)(2,1)S(1)}, bf16[256,384]{1,0:T(8,128)(2,1)S(1)}, bf16[256,384]{1,0:T(8,128)(2,1)S(1)}) custom-call(bf16[512,384]{1,0:T(8,128)(2,1)S(1)} %get-tuple-element.39.xpad_ref, f32[8,512]{1,0:T(8,128)S(1)} %get-tuple-element.40.wet_ref, ...), custom_call_target="tpu_custom_call" | custom-call | flops 679477248 | bytes 2654208 | tf_op jit(solution)/shard_map/first/pallas_call | solution.py:30
  28.8 1.3 %collective-permute-start.7 = (bf16[256,384]{1,0:T(8,128)(2,1)S(1)}, bf16[256,384]{1,0:T(8,128)(2,1)S(1)}, u32[]{:S(2)}, u32[]{:S(2)}) collective-permute-start(bf16[256,384]{1,0:T(8,128)(2,1)S(1)} %get-tuple-element.44.give_ref), channel_id=1, source_target_pairs={{0,16},{16,0},{1,17},{17,1},{2,18},{18,2},{3,19},{19,3},{4,20},{20... | collective-permute-start | bytes 589832 | tf_op jit(solution)/shard_map/ppermute | solution.py:444
  30.1 4.4 %collective-permute-done.7.refs_4_ = bf16[256,384]{1,0:T(8,128)(2,1)S(1)} collective-permute-done((bf16[256,384]{1,0:T(8,128)(2,1)S(1)}, bf16[256,384]{1,0:T(8,128)(2,1)S(1)}, u32[]{:S(2)}, u32[]{:S(2)}) %collective-permute-start.7) | collective-permute-done | bytes 196640 | tf_op jit(solution)/shard_map/ppermute | solution.py:444
  34.5 4.1 %grads.1 = (bf16[8,272,384]{2,1,0:T(8,128)(2,1)S(1)}, bf16[8,272,384]{2,1,0:T(8,128)(2,1)}) custom-call(bf16[512,384]{1,0:T(8,128)(2,1)S(1)} %collective-permute-done.6.refs_0_, bf16[512,384]{1,0:T(8,128)(2,1)S(1)} %get-tuple-element.47.upad_ref.refs_1_, bf16[512,384]{1,0:T(8,128)(2,1)S(1)} %get-tuple-element.42.gpad_ref.refs_2_, ...), custom_call_target="tpu_custom_call" | custom-call | flops 1358954496 | bytes 3342336 | tf_op jit(solution)/shard_map/grads/pallas_call | solution.py:30
  38.6 2.1 %collective-permute-start.8 = (bf16[8,272,384]{2,1,0:T(8,128)(2,1)}, bf16[8,272,384]{2,1,0:T(8,128)(2,1)S(1)}, u32[]{:S(2)}, u32[]{:S(2)}) collective-permute-start(bf16[8,272,384]{2,1,0:T(8,128)(2,1)} %get-tuple-element.53), channel_id=1, source_target_pairs={{0,1},{1,0},{2,3},{3,2},{4,5},{5,4},{6,7},{7,6},{8,9},{9,8},{10,11... | collective-permute-start | bytes 5013512 | tf_op jit(solution)/shard_map/ppermute | solution.py:444
  40.7 3.4 %collective-permute-done.8 = bf16[8,272,384]{2,1,0:T(8,128)(2,1)S(1)} collective-permute-done((bf16[8,272,384]{2,1,0:T(8,128)(2,1)}, bf16[8,272,384]{2,1,0:T(8,128)(2,1)S(1)}, u32[]{:S(2)}, u32[]{:S(2)}) %collective-permute-start.8) | collective-permute-done | bytes 1671200 | tf_op jit(solution)/shard_map/ppermute | solution.py:444
  44.1 1.2 %copy-done.7 = bf16[8,272,384]{2,1,0:T(8,128)(2,1)} copy-done((bf16[8,272,384]{2,1,0:T(8,128)(2,1)}, bf16[8,272,384]{2,1,0:T(8,128)(2,1)S(1)}, u32[]{:S(2)}) %copy-start.7) | copy-done | bytes 1671192
  45.3 1.8 %split.1 = (bf16[4,1,144,384]{3,2,1,0:T(8,128)(2,1)S(1)}, bf16[4,1,144,384]{3,2,1,0:T(8,128)(2,1)S(1)}, bf16[2,2,128,384]{3,2,1,0:T(8,128)(2,1)S(1)}, bf16[2,2,128,384]{3,2,1,0:T(8,128)(2,1)S(1)}) custom-call(bf16[4,2,1,272,384]{4,3,2,1,0:T(8,128)(2,1)S(1)} %bitcast.26, bf16[4,2,1,272,384]{4,3,2,1,0:T(8,128)(2,1)} %bitcast.47), custom_call_target="tpu_custom_call" | custom-call | bytes 5013504 | tf_op jit(solution)/shard_map/split/pallas_call | solution.py:30
  47.1 3.9 %collective-permute-start.9 = (bf16[4,1,144,384]{3,2,1,0:T(8,128)(2,1)S(1)}, bf16[4,1,144,384]{3,2,1,0:T(8,128)(2,1)S(1)}, u32[]{:S(2)}, u32[]{:S(2)}) collective-permute-start(bf16[4,1,144,384]{3,2,1,0:T(8,128)(2,1)S(1)} %get-tuple-element.55), channel_id=1, source_target_pairs={{0,2},{1,3},{2,0},{3,1},{4,6},{5,7},{6,4},{7,5},{8,10},{9,11},{10,... | collective-permute-start | bytes 1327112 | tf_op jit(solution)/shard_map/ppermute | solution.py:444
  51.0 1.6 %collective-permute-start.12 = (bf16[2,2,128,384]{3,2,1,0:T(8,128)(2,1)S(1)}, bf16[2,2,128,384]{3,2,1,0:T(8,128)(2,1)S(1)}, u32[]{:S(2)}, u32[]{:S(2)}) collective-permute-start(bf16[2,2,128,384]{3,2,1,0:T(8,128)(2,1)S(1)} %get-tuple-element.61), channel_id=1, source_target_pairs={{0,4},{1,5},{2,6},{3,7},{4,0},{5,1},{6,2},{7,3},{8,12},{9,13},{10,... | collective-permute-start | bytes 1179656 | tf_op jit(solution)/shard_map/ppermute | solution.py:444
  52.6 9.1 %collective-permute-done.9 = bf16[4,1,144,384]{3,2,1,0:T(8,128)(2,1)S(1)} collective-permute-done((bf16[4,1,144,384]{3,2,1,0:T(8,128)(2,1)S(1)}, bf16[4,1,144,384]{3,2,1,0:T(8,128)(2,1)S(1)}, u32[]{:S(2)}, u32[]{:S(2)}) %collective-permute-start.9) | collective-permute-done | bytes 442400 | tf_op jit(solution)/shard_map/ppermute | solution.py:444
  61.8 2.3 %collective-permute-start.10 = (bf16[2,1,144,384]{3,2,0,1:T(8,128)(2,1)S(1)}, bf16[2,1,144,384]{3,2,0,1:T(8,128)(2,1)S(1)}, u32[]{:S(2)}, u32[]{:S(2)}) collective-permute-start(bf16[2,1,144,384]{3,2,0,1:T(8,128)(2,1)S(1)} %bitcast.43), channel_id=1, source_target_pairs={{0,4},{1,5},{2,6},{3,7},{4,0},{5,1},{6,2},{7,3},{8,12},{9,13},{10,... | collective-permute-start | bytes 663560 | tf_op jit(solution)/shard_map/ppermute | solution.py:444
  64.2 2.7 %collective-permute-start.13 = (bf16[1,2,128,384]{3,2,1,0:T(8,128)(2,1)S(1)}, bf16[1,2,128,384]{3,2,1,0:T(8,128)(2,1)S(1)}, u32[]{:S(2)}, u32[]{:S(2)}) collective-permute-start(bf16[1,2,128,384]{3,2,1,0:T(8,128)(2,1)S(1)} %get-tuple-element.63), channel_id=1, source_target_pairs={{0,8},{1,9},{2,10},{3,11},{4,12},{5,13},{6,14},{7,15},{8,0},{9,1},... | collective-permute-start | bytes 589832 | tf_op jit(solution)/shard_map/ppermute | solution.py:444
  66.9 1.3 %collective-permute-start.3 = (bf16[256,384]{1,0:T(8,128)(2,1)S(1)}, bf16[256,384]{1,0:T(8,128)(2,1)S(1)}, u32[]{:S(2)}, u32[]{:S(2)}) collective-permute-start(bf16[256,384]{1,0:T(8,128)(2,1)S(1)} %get-tuple-element.45), channel_id=1, source_target_pairs={{0,1},{1,2},{2,3},{3,4},{4,5},{5,6},{6,7},{7,8},{8,9},{9,10},{10,1... | collective-permute-start | bytes 589832 | tf_op jit(solution)/shard_map/ppermute | solution.py:451
  68.2 1.5 %collective-permute-start.4 = (bf16[256,384]{1,0:T(8,128)(2,1)S(1)}, bf16[256,384]{1,0:T(8,128)(2,1)S(1)}, u32[]{:S(2)}, u32[]{:S(2)}) collective-permute-start(bf16[256,384]{1,0:T(8,128)(2,1)S(1)} %get-tuple-element.46), channel_id=1, source_target_pairs={{1,0},{2,1},{3,2},{4,3},{5,4},{6,5},{7,6},{8,7},{9,8},{10,9},{11,1... | collective-permute-start | bytes 589832 | tf_op jit(solution)/shard_map/ppermute | solution.py:451
  69.7 3.0 %collective-permute-done.13 = bf16[1,2,128,384]{3,2,1,0:T(8,128)(2,1)S(1)} collective-permute-done((bf16[1,2,128,384]{3,2,1,0:T(8,128)(2,1)S(1)}, bf16[1,2,128,384]{3,2,1,0:T(8,128)(2,1)S(1)}, u32[]{:S(2)}, u32[]{:S(2)}) %collective-permute-start.13) | collective-permute-done | bytes 196640 | tf_op jit(solution)/shard_map/ppermute | solution.py:444
  72.7 2.8 %collective-permute-start.14 = (bf16[1,1,128,384]{3,2,1,0:T(8,128)(2,1)S(1)}, bf16[1,1,128,384]{3,2,1,0:T(8,128)(2,1)S(1)}, u32[]{:S(2)}, u32[]{:S(2)}) collective-permute-start(bf16[1,1,128,384]{3,2,1,0:T(8,128)(2,1)S(1)} %get-tuple-element.65), channel_id=1, source_target_pairs={{0,2},{1,3},{2,0},{3,1},{4,6},{5,7},{6,4},{7,5},{8,10},{9,11},{10,... | collective-permute-start | bytes 294920 | tf_op jit(solution)/shard_map/ppermute | solution.py:444
  75.5 3.4 %collective-permute-start.11 = (bf16[1,1,144,384]{3,2,1,0:T(8,128)(2,1)S(1)}, bf16[1,1,144,384]{3,2,1,0:T(8,128)(2,1)S(1)}, u32[]{:S(2)}, u32[]{:S(2)}) collective-permute-start(bf16[1,1,144,384]{3,2,1,0:T(8,128)(2,1)S(1)} %get-tuple-element.59), channel_id=1, source_target_pairs={{0,8},{1,9},{2,10},{3,11},{4,12},{5,13},{6,14},{7,15},{8,0},{9,1},... | collective-permute-start | bytes 331784 | tf_op jit(solution)/shard_map/ppermute | solution.py:444
  79.0 6.0 %next.1 = (bf16[2,128,384]{2,1,0:T(8,128)(2,1)}, f32[256,384]{1,0:T(8,128)S(1)}, f32[4,256]{1,0:T(4,128)S(1)}) custom-call(bf16[256,384]{1,0:T(8,128)(2,1)S(1)} %get-tuple-element.43.stay_ref.refs_3_, bf16[256,384]{1,0:T(8,128)(2,1)S(1)} %get-tuple-element.44.give_ref, bf16[256,384]{1,0:T(8,128)(2,1)S(1)} %collective-permute-done.3.low_ref, ...), custom_call_target="tpu_custom_call" | custom-call | flops 1358954496 | bytes 5308416 | tf_op jit(solution)/shard_map/next/pallas_call | solution.py:30
  85.5 3.1 %collective-permute-done.5.arrived_ref = f32[4,256]{1,0:T(4,128)S(1)} collective-permute-done((f32[4,256]{1,0:T(4,128)S(1)}, f32[4,256]{1,0:T(4,128)S(1)}, u32[]{:S(2)}, u32[]{:S(2)}) %collective-permute-start.5) | collective-permute-done | bytes 4128 | tf_op jit(solution)/shard_map/ppermute | solution.py:444
  88.6 1.2 %last.1 = bf16[2,128,384]{2,1,0:T(8,128)(2,1)} custom-call(f32[256,384]{1,0:T(8,128)S(1)} %get-tuple-element.49.grad_ref, f32[4,256]{1,0:T(4,128)S(1)} %collective-permute-done.5.arrived_ref, f32[8,512]{1,0:T(8,128)S(1)} %get-tuple-element.40.wet_ref, f32[16,384]{1,0:T(8,128)S(1)} %fusion.9.terms_ref), custom_call_target="tpu_custom_call" | custom-call | tf_op jit(solution)/shard_map/last/pallas_call | solution.py:30
  (30 shorter events, 4.5 us)
Async XLA Ops:
  0.6 0.9 %copy-start.1 = (bf16[1,2,128,384]{3,2,1,0:T(8,128)(2,1)S(1)}, bf16[1,2,128,384]{3,2,1,0:T(8,128)(2,1)}, u32[]{:S(2)}) copy-start(bf16[1,2,128,384]{3,2,1,0:T(8,128)(2,1)} %param.10) | copy-start | bytes 589828
  1.6 0.9 %copy-start.3 = (bf16[1,2,128,384]{3,2,1,0:T(8,128)(2,1)S(1)}, bf16[1,2,128,384]{3,2,1,0:T(8,128)(2,1)}, u32[]{:S(2)}) copy-start(bf16[1,2,128,384]{3,2,1,0:T(8,128)(2,1)} %param.11) | copy-start | bytes 589828
  2.5 0.7 copy-start.6
  3.3 4.5 %collective-permute-start = (bf16[272,384]{1,0:T(8,128)(2,1)S(1)}, bf16[272,384]{1,0:T(8,128)(2,1)S(1)}, u32[]{:S(2)}, u32[]{:S(2)}) collective-permute-start(bf16[272,384]{1,0:T(8,128)(2,1)S(1)} %get-tuple-element.36), channel_id=1, source_target_pairs={{0,1},{1,2},{2,3},{3,4},{4,5},{5,6},{6,7},{7,8},{8,9},{9,10},{10,1... | collective-permute-start | bytes 626696 | tf_op jit(solution)/shard_map/ppermute | solution.py:451
  5.7 5.5 %collective-permute-start.1 = (bf16[272,384]{1,0:T(8,128)(2,1)S(1)}, bf16[272,384]{1,0:T(8,128)(2,1)S(1)}, u32[]{:S(2)}, u32[]{:S(2)}) collective-permute-start(bf16[272,384]{1,0:T(8,128)(2,1)S(1)} %get-tuple-element.37), channel_id=1, source_target_pairs={{1,0},{2,1},{3,2},{4,3},{5,4},{6,5},{7,6},{8,7},{9,8},{10,9},{11,1... | collective-permute-start | bytes 626696 | tf_op jit(solution)/shard_map/ppermute | solution.py:451
  11.2 0.9 %copy-start.2 = (bf16[1,2,128,384]{3,2,1,0:T(8,128)(2,1)S(1)}, bf16[1,2,128,384]{3,2,1,0:T(8,128)(2,1)}, u32[]{:S(2)}) copy-start(bf16[1,2,128,384]{3,2,1,0:T(8,128)(2,1)} %param.10) | copy-start | bytes 589828
  12.1 0.9 %copy-start.4 = (bf16[1,2,128,384]{3,2,1,0:T(8,128)(2,1)S(1)}, bf16[1,2,128,384]{3,2,1,0:T(8,128)(2,1)}, u32[]{:S(2)}) copy-start(bf16[1,2,128,384]{3,2,1,0:T(8,128)(2,1)} %param.11) | copy-start | bytes 589828
  13.3 21.2 %collective-permute-start.6 = (bf16[512,384]{1,0:T(8,128)(2,1)S(1)}, bf16[512,384]{1,0:T(8,128)(2,1)S(1)}, u32[]{:S(2)}, u32[]{:S(2)}) collective-permute-start(bf16[512,384]{1,0:T(8,128)(2,1)S(1)} %get-tuple-element.51), channel_id=1, source_target_pairs={{0,16},{16,0},{1,17},{17,1},{2,18},{18,2},{3,19},{19,3},{4,20},{20... | collective-permute-start | bytes 1179656 | tf_op jit(solution)/shard_map/ppermute | solution.py:444
  14.9 1.5 %copy-start = (bf16[2,3,3,192,192]{4,3,2,1,0:T(8,128)(2,1)S(1)}, bf16[2,3,3,192,192]{4,3,2,1,0:T(8,128)(2,1)}, u32[]{:S(2)}) copy-start(bf16[2,3,3,192,192]{4,3,2,1,0:T(8,128)(2,1)} %param.12) | copy-start | bytes 3981316
  21.5 3.8 %collective-permute-start.2 = (f32[4,512]{1,0:T(4,128)S(1)}, f32[4,512]{1,0:T(4,128)S(1)}, u32[]{:S(2)}, u32[]{:S(2)}) collective-permute-start(f32[4,512]{1,0:T(4,128)S(1)} %get-tuple-element.41.refs_5_), channel_id=1, source_target_pairs={{0,16},{16,0},{1,17},{17,1},{2,18},{18,2},{3,19},{19,3},{4,20},{20... | collective-permute-start | bytes 24584 | tf_op jit(solution)/shard_map/ppermute | solution.py:444
  25.3 9.2 %copy-start.5 = (bf16[4,384]{1,0:T(4,128)(2,1)S(1)}, bf16[4,384]{1,0:T(4,128)(2,1)}, u32[]{:S(2)}) copy-start(bf16[4,384]{1,0:T(4,128)(2,1)} %refs_6_.1) | copy-start | bytes 9220
  28.8 5.7 %collective-permute-start.7 = (bf16[256,384]{1,0:T(8,128)(2,1)S(1)}, bf16[256,384]{1,0:T(8,128)(2,1)S(1)}, u32[]{:S(2)}, u32[]{:S(2)}) collective-permute-start(bf16[256,384]{1,0:T(8,128)(2,1)S(1)} %get-tuple-element.44.give_ref), channel_id=1, source_target_pairs={{0,16},{16,0},{1,17},{17,1},{2,18},{18,2},{3,19},{19,3},{4,20},{20... | collective-permute-start | bytes 589832 | tf_op jit(solution)/shard_map/ppermute | solution.py:444
  38.6 5.5 %collective-permute-start.8 = (bf16[8,272,384]{2,1,0:T(8,128)(2,1)}, bf16[8,272,384]{2,1,0:T(8,128)(2,1)S(1)}, u32[]{:S(2)}, u32[]{:S(2)}) collective-permute-start(bf16[8,272,384]{2,1,0:T(8,128)(2,1)} %get-tuple-element.53), channel_id=1, source_target_pairs={{0,1},{1,0},{2,3},{3,2},{4,5},{5,4},{6,7},{7,6},{8,9},{9,8},{10,11... | collective-permute-start | bytes 5013512 | tf_op jit(solution)/shard_map/ppermute | solution.py:444
  44.1 1.2 %copy-start.7 = (bf16[8,272,384]{2,1,0:T(8,128)(2,1)}, bf16[8,272,384]{2,1,0:T(8,128)(2,1)S(1)}, u32[]{:S(2)}) copy-start(bf16[8,272,384]{2,1,0:T(8,128)(2,1)S(1)} %collective-permute-done.8) | copy-start | bytes 5013508
  47.1 14.6 %collective-permute-start.9 = (bf16[4,1,144,384]{3,2,1,0:T(8,128)(2,1)S(1)}, bf16[4,1,144,384]{3,2,1,0:T(8,128)(2,1)S(1)}, u32[]{:S(2)}, u32[]{:S(2)}) collective-permute-start(bf16[4,1,144,384]{3,2,1,0:T(8,128)(2,1)S(1)} %get-tuple-element.55), channel_id=1, source_target_pairs={{0,2},{1,3},{2,0},{3,1},{4,6},{5,7},{6,4},{7,5},{8,10},{9,11},{10,... | collective-permute-start | bytes 1327112 | tf_op jit(solution)/shard_map/ppermute | solution.py:444
  51.0 13.1 %collective-permute-start.12 = (bf16[2,2,128,384]{3,2,1,0:T(8,128)(2,1)S(1)}, bf16[2,2,128,384]{3,2,1,0:T(8,128)(2,1)S(1)}, u32[]{:S(2)}, u32[]{:S(2)}) collective-permute-start(bf16[2,2,128,384]{3,2,1,0:T(8,128)(2,1)S(1)} %get-tuple-element.61), channel_id=1, source_target_pairs={{0,4},{1,5},{2,6},{3,7},{4,0},{5,1},{6,2},{7,3},{8,12},{9,13},{10,... | collective-permute-start | bytes 1179656 | tf_op jit(solution)/shard_map/ppermute | solution.py:444
  61.8 13.6 %collective-permute-start.10 = (bf16[2,1,144,384]{3,2,0,1:T(8,128)(2,1)S(1)}, bf16[2,1,144,384]{3,2,0,1:T(8,128)(2,1)S(1)}, u32[]{:S(2)}, u32[]{:S(2)}) collective-permute-start(bf16[2,1,144,384]{3,2,0,1:T(8,128)(2,1)S(1)} %bitcast.43), channel_id=1, source_target_pairs={{0,4},{1,5},{2,6},{3,7},{4,0},{5,1},{6,2},{7,3},{8,12},{9,13},{10,... | collective-permute-start | bytes 663560 | tf_op jit(solution)/shard_map/ppermute | solution.py:444
  64.2 8.4 %collective-permute-start.13 = (bf16[1,2,128,384]{3,2,1,0:T(8,128)(2,1)S(1)}, bf16[1,2,128,384]{3,2,1,0:T(8,128)(2,1)S(1)}, u32[]{:S(2)}, u32[]{:S(2)}) collective-permute-start(bf16[1,2,128,384]{3,2,1,0:T(8,128)(2,1)S(1)} %get-tuple-element.63), channel_id=1, source_target_pairs={{0,8},{1,9},{2,10},{3,11},{4,12},{5,13},{6,14},{7,15},{8,0},{9,1},... | collective-permute-start | bytes 589832 | tf_op jit(solution)/shard_map/ppermute | solution.py:444
  66.9 12.1 %collective-permute-start.3 = (bf16[256,384]{1,0:T(8,128)(2,1)S(1)}, bf16[256,384]{1,0:T(8,128)(2,1)S(1)}, u32[]{:S(2)}, u32[]{:S(2)}) collective-permute-start(bf16[256,384]{1,0:T(8,128)(2,1)S(1)} %get-tuple-element.45), channel_id=1, source_target_pairs={{0,1},{1,2},{2,3},{3,4},{4,5},{5,6},{6,7},{7,8},{8,9},{9,10},{10,1... | collective-permute-start | bytes 589832 | tf_op jit(solution)/shard_map/ppermute | solution.py:451
  68.2 10.8 %collective-permute-start.4 = (bf16[256,384]{1,0:T(8,128)(2,1)S(1)}, bf16[256,384]{1,0:T(8,128)(2,1)S(1)}, u32[]{:S(2)}, u32[]{:S(2)}) collective-permute-start(bf16[256,384]{1,0:T(8,128)(2,1)S(1)} %get-tuple-element.46), channel_id=1, source_target_pairs={{1,0},{2,1},{3,2},{4,3},{5,4},{6,5},{7,6},{8,7},{9,8},{10,9},{11,1... | collective-permute-start | bytes 589832 | tf_op jit(solution)/shard_map/ppermute | solution.py:451
  72.7 17.1 %collective-permute-start.14 = (bf16[1,1,128,384]{3,2,1,0:T(8,128)(2,1)S(1)}, bf16[1,1,128,384]{3,2,1,0:T(8,128)(2,1)S(1)}, u32[]{:S(2)}, u32[]{:S(2)}) collective-permute-start(bf16[1,1,128,384]{3,2,1,0:T(8,128)(2,1)S(1)} %get-tuple-element.65), channel_id=1, source_target_pairs={{0,2},{1,3},{2,0},{3,1},{4,6},{5,7},{6,4},{7,5},{8,10},{9,11},{10,... | collective-permute-start | bytes 294920 | tf_op jit(solution)/shard_map/ppermute | solution.py:444
  75.5 14.3 %collective-permute-start.11 = (bf16[1,1,144,384]{3,2,1,0:T(8,128)(2,1)S(1)}, bf16[1,1,144,384]{3,2,1,0:T(8,128)(2,1)S(1)}, u32[]{:S(2)}, u32[]{:S(2)}) collective-permute-start(bf16[1,1,144,384]{3,2,1,0:T(8,128)(2,1)S(1)} %get-tuple-element.59), channel_id=1, source_target_pairs={{0,8},{1,9},{2,10},{3,11},{4,12},{5,13},{6,14},{7,15},{8,0},{9,1},... | collective-permute-start | bytes 331784 | tf_op jit(solution)/shard_map/ppermute | solution.py:444
  85.0 3.7 %collective-permute-start.5 = (f32[4,256]{1,0:T(4,128)S(1)}, f32[4,256]{1,0:T(4,128)S(1)}, u32[]{:S(2)}, u32[]{:S(2)}) collective-permute-start(f32[4,256]{1,0:T(4,128)S(1)} %get-tuple-element.50), channel_id=1, source_target_pairs={{0,16},{16,0},{1,17},{17,1},{2,18},{18,2},{3,19},{19,3},{4,20},{20... | collective-permute-start | bytes 12296 | tf_op jit(solution)/shard_map/ppermute | solution.py:444
where the time goes:
time: 91.2 us; the launch traced here: 90.7 us
  starting transfers between devices  28.6 us (31%)
  waiting for transfers between devices  27.1 us (30%)
  Pallas kernels  26.3 us (29%)
  local copies, waits for them, and re-layouts  7.06 us (8%)
    pallas_call x14, Pallas kernels, call(): pl.pallas_call(kernel, out_shape=outs, in_specs=in_specs or [WHOLE] * len...  26.3 us
    ppermute x11, waiting for transfers between devices, swapped(): return lax.ppermute(value, axis, pairs)  23.8 us
    ppermute x11, starting transfers between devices, swapped(): return lax.ppermute(value, axis, pairs)  22.2 us
    unnamed x16, local copies, waits for them, and re-layouts  7.06 us
    ppermute x2, starting transfers between devices, halo(): lax.ppermute(up, 'lat', forward)  3.65 us
    ppermute x2, waiting for transfers between devices, halo(): lax.ppermute(down, 'lat', backward)  3.3 us
    ppermute x2, starting transfers between devices, halo(): lax.ppermute(down, 'lat', backward)  2.76 us
  transfers between devices with their start and end apart: 15, of which 7 were waited for; matrix products, arithmetic and copies ran while one was open for 1% of the time, Pallas kernels for 21%

commit v1 on v0

v1 whole, which is shorter than its diff:
```python
import functools
import math

import jax
import jax.numpy as jnp
from jax import lax
from jax.experimental import pallas as pl
from jax.experimental.pallas import tpu as pltpu
from jax.sharding import PartitionSpec as P

HIGHEST = lax.Precision.HIGHEST
GELU_SCALE = 0.7978845608028654
GELU_CUBIC = 0.044715
F32 = jnp.float32
BF16 = jnp.bfloat16
WHOLE = pl.BlockSpec(memory_space=pltpu.VMEM)
IN_PLACE = pl.BlockSpec(memory_space=pltpu.HBM)
ANYWHERE = pl.BlockSpec(memory_space=pl.ANY)
VMEM_LIMIT = 32 * 1024 * 1024
MOST_VMEM = 52 * 1024 * 1024
PACE = 8
PACK_VMEM = 62 * 1024 * 1024

NN = (((1,), (0,)), ((), ()))
NT = (((1,), (1,)), ((), ()))
TN = (((0,), (0,)), ((), ()))


def shape(dims, kind):
    return jax.ShapeDtypeStruct(dims, kind)


def call(kernel, outs, inputs, in_specs=None, scratch=(), flops=0, moved=0, name=None, limit=VMEM_LIMIT, out_spec=WHOLE):
    return pl.pallas_call(
        kernel,
        out_shape=outs,
        in_specs=in_specs or [WHOLE] * len(inputs),
        out_specs=jax.tree.map(lambda _: out_spec, outs),
        scratch_shapes=list(scratch),
        compiler_params=pltpu.CompilerParams(vmem_limit_bytes=limit),
        cost_estimate=pl.CostEstimate(flops=flops, bytes_accessed=moved, transcendentals=0),
        name=name,
    )(*inputs)


def on_ocean():
    return lax.axis_index("grp") == 0


def dot(left, right, dims=NN, precision=None):
    return lax.dot_general(left, right, dims, precision=precision, preferred_element_type=F32)


def moved_cells(values, axis, cols):
    count = values.shape[axis]
    place = lax.rem(lax.broadcasted_iota(jnp.int32, values.shape, axis), cols)
    before = jnp.where(place == 0, 0.0, pltpu.roll(values, 1, axis))
    after = jnp.where(place == cols - 1, 0.0, pltpu.roll(values, count - 1, axis))
    return before, after


def wet_halves(wet, cols, channels):
    source = lax.broadcasted_iota(jnp.int32, (2 * cols, 2 * cols), 0)
    target = lax.broadcasted_iota(jnp.int32, (2 * cols, 2 * cols), 1)
    wanted = 2 * lax.rem(target, cols) + jnp.where(target >= cols, 1, 0)
    chooser = (source == wanted).astype(F32).astype(BF16)
    padded = jnp.concatenate([wet.astype(F32), jnp.zeros((14, 2 * cols), F32)], axis=0)
    apart = dot(padded.astype(BF16), chooser)
    return jnp.concatenate([apart, jnp.zeros((16, channels - 2 * cols), F32)], axis=1)


def pack_kernel(x_any, g_any, wet_any, up_any, down_any, wet_ref, edge_ref, wet_sem, sems, *, cols):
    fetch = pltpu.make_async_copy(wet_any, wet_ref, wet_sem)
    fetch.start()
    copies = []
    for row, out_any in ((1, up_any), (0, down_any)):
        for part, source in enumerate((x_any, g_any)):
            target = out_any.at[pl.ds(part * cols, cols), :]
            copies.append(pltpu.make_async_copy(source.at[row], target, sems.at[row, part]))
            copies[-1].start()
    fetch.wait()
    wide = wet_halves(wet_ref[...], cols, edge_ref.shape[2])
    edge_ref[0] = wide.astype(BF16)
    edge_ref[1] = pltpu.roll(wide, 15, 0).astype(BF16)
    for row, out_any in ((1, up_any), (0, down_any)):
        target = out_any.at[pl.ds(2 * cols, 16), :]
        copies.append(pltpu.make_async_copy(edge_ref.at[row], target, sems.at[row, 2]))
        copies[-1].start()
    for copy in copies:
        copy.wait()


def hold_kernel(x_any, g_any, wet_any, x_ref, g_ref, own_ref, wet_ref, sems, *, cols):
    pairs = ((wet_any, wet_ref), (x_any, x_ref), (g_any, g_ref))
    copies = [pltpu.make_async_copy(*pair, sems.at[index]) for index, pair in enumerate(pairs)]
    for copy in copies:
        copy.start()
    copies[0].wait()
    own_ref[...] = wet_halves(wet_ref[...], cols, own_ref.shape[1]).astype(BF16)
    copies[1].wait()
    copies[2].wait()


def outgoing_kernel(
    x_ref, g_ref, low_ref, high_ref, own_ref, terms_ref,
    xpad_ref, gpad_ref, wet_ref, early_ref, sent_ref, *, cols,
):
    for pad_ref, own, start in ((xpad_ref, x_ref, 0), (gpad_ref, g_ref, cols)):
        pad_ref[0:cols, :] = low_ref[start : start + cols, :]
        pad_ref[cols : 2 * cols, :] = own[0]
        pad_ref[2 * cols : 3 * cols, :] = own[1]
        pad_ref[3 * cols : 4 * cols, :] = high_ref[start : start + cols, :]
    low_wet = low_ref[2 * cols :, :].astype(F32)
    high_wet = high_ref[2 * cols :, :].astype(F32)
    own_wet = own_ref[...].astype(F32)
    halves = []
    for start in (0, cols):
        lanes = slice(start, start + cols)
        rows = (low_wet[0:1, lanes], own_wet[0:1, lanes], own_wet[1:2, lanes], high_wet[0:1, lanes])
        halves.append(jnp.concatenate(rows, axis=1))
    first_wet, second_wet = halves
    inverse = 1.0 / jnp.maximum(first_wet + second_wet, 1.0)
    wet_ref[0:1, :] = first_wet
    wet_ref[1:2, :] = second_wet
    wet_ref[2:3, :] = inverse
    wet_ref[3:8, :] = jnp.zeros((5, 4 * cols), F32)
    xpad = xpad_ref[...]
    projected = dot(terms_ref[0:8, :].astype(BF16), xpad, NT)
    mixed = (projected[0:4] * first_wet + projected[4:8] * second_wet) * inverse
    sent_ref[...] = jnp.where(on_ocean(), mixed, projected[0:4])
    early_ref[...] = jnp.where(on_ocean(), gpad_ref[...], xpad)


def halves_apart(values, narrow):
    wide = -(-narrow // 128) * 128
    lane = lax.broadcasted_iota(jnp.int32, values.shape, 1)
    even = jnp.where(lane < narrow, values, 0.0)
    odd = jnp.where(lane < narrow, pltpu.roll(values, narrow, 1), 0.0)
    return even[:, :wide], odd[:, :wide]


def halves_with_columns(pad, cols):
    even, odd = halves_apart(pad.astype(F32), pad.shape[1] // 2)
    odd_before = moved_cells(odd, 0, cols)[0].astype(BF16)
    even_after = moved_cells(even, 0, cols)[1].astype(BF16)
    even, odd = even.astype(BF16), odd.astype(BF16)
    return (odd_before, even, odd), (even, odd, even_after)


def with_columns(pad, cols):
    before, after = moved_cells(pad.astype(F32), 0, cols)
    return before.astype(BF16), pad, after.astype(BF16)


def conv_scratch(channels):
    narrow = channels // 2
    wide = -(-narrow // 128) * 128
    return [
        pltpu.VMEM((9, channels, channels), BF16),
        pltpu.VMEM((9, wide, narrow), BF16),
        pltpu.SemaphoreType.DMA((3,)),
    ]


def convolve(pad_ref, out_ref, atmos_ref, ocean_ref, layer, flipped, scratch, cols, meanwhile=None):
    atmos_buffer, ocean_buffer, sems = scratch
    order = (2, 1, 0) if flipped else (0, 1, 2)
    channels = atmos_buffer.shape[2]
    narrow = ocean_buffer.shape[2]
    rows = out_ref.shape[0]

    def atmos_copy(group):
        taps = pl.ds(9 * layer + 3 * group, 3)
        return pltpu.make_async_copy(atmos_ref.at[taps], atmos_buffer.at[pl.ds(3 * group, 3)], sems.at[group])

    def ocean_copy(group):
        taps = pl.ds(9 * layer + 3 * group, 3)
        target = ocean_buffer.at[pl.ds(3 * group, 3), pl.ds(0, narrow), :]
        return pltpu.make_async_copy(ocean_ref.at[taps], target, sems.at[group])

    @pl.when(on_ocean())
    def _():
        for group in order:
            ocean_copy(group).start()
        gap = ocean_buffer.shape[1] - narrow
        if gap:
            ocean_buffer[:, narrow:, :] = jnp.zeros((9, gap, narrow), BF16)
        if meanwhile is not None:
            meanwhile()
        evens, odds = halves_with_columns(pad_ref[...], cols)
        total = None
        if not flipped:
            even, odd = jnp.concatenate(evens, axis=1), jnp.concatenate(odds, axis=1)
        for row_tap, group in enumerate(order):
            ocean_copy(group).wait()
            span = slice(cols * row_tap, cols * row_tap + rows)
            if flipped:
                part = None
                for col_tap in range(3):
                    left = jnp.concatenate([evens[col_tap][span], odds[col_tap][span]], axis=0)
                    kernel = ocean_buffer[8 - (3 * row_tap + col_tap), 0:narrow, :]
                    piece = dot(left[:, :narrow], kernel, NT)
                    part = piece if part is None else part + piece
            else:
                kernel = ocean_buffer[3 * group : 3 * group + 3].reshape(3 * ocean_buffer.shape[1], narrow)
                part = dot(jnp.concatenate([even[span], odd[span]], axis=0), kernel)
            total = part if total is None else total + part
        out_ref[...] = jnp.concatenate([total[:rows], total[rows:]], axis=1)

    @pl.when(jnp.logical_not(on_ocean()))
    def _():
        for group in order:
            atmos_copy(group).start()
        if meanwhile is not None:
            meanwhile()
        taps = with_columns(pad_ref[...], cols)
        total = None
        if not flipped:
            joined = jnp.concatenate(taps, axis=1)
        for row_tap, group in enumerate(order):
            atmos_copy(group).wait()
            span = slice(cols * row_tap, cols * row_tap + rows)
            if flipped:
                part = None
                for col_tap in range(3):
                    piece = dot(taps[col_tap][span], atmos_buffer[8 - (3 * row_tap + col_tap)], NT)
                    part = piece if part is None else part + piece
            else:
                kernel = atmos_buffer[3 * group : 3 * group + 3].reshape(3 * channels, channels)
                part = dot(joined[span], kernel)
            total = part if total is None else total + part
        out_ref[...] = total


def back_kernel(gpad_ref, atmos_ref, ocean_ref, out_ref, *scratch, cols):
    convolve(gpad_ref, out_ref, atmos_ref, ocean_ref, 1, True, scratch, cols)


def spread(arrived, wet, mixing, terms):
    first_wet, second_wet = wet
    both = jnp.concatenate([arrived * first_wet, arrived * second_wet], axis=0)
    alone = jnp.concatenate([arrived, jnp.zeros_like(arrived)], axis=0)
    return dot(jnp.where(mixing, both, alone), terms, TN, HIGHEST)


def first_kernel(
    xpad_ref, wet_ref, arrived_ref, terms_ref, back_ref, atmos_ref, ocean_ref,
    u_ref, stay_ref, give_ref, up_ref, down_ref, first_ref, *scratch, cols,
):
    def couple():
        wet = wet_ref[0:1, :], wet_ref[1:2, :]
        coupled = spread(arrived_ref[...], wet, on_ocean(), terms_ref[8:16, :])
        u_ref[...] = (xpad_ref[...].astype(F32) + coupled).astype(BF16)

    convolve(u_ref, first_ref, atmos_ref, ocean_ref, 0, False, scratch, cols, couple)
    first = first_ref[...]
    tangent = jnp.tanh(GELU_SCALE * (first + GELU_CUBIC * first * first * first))
    hidden = (0.5 * first * (1.0 + tangent)).astype(BF16)
    slope = 0.5 * (1.0 + tangent) + 0.5 * first * (1.0 - tangent * tangent) * GELU_SCALE * (
        1.0 + 3.0 * GELU_CUBIC * first * first
    )
    first_grad = (back_ref[...] * slope).astype(BF16)
    stay_ref[...] = jnp.where(on_ocean(), first_grad, hidden)
    give_ref[...] = jnp.where(on_ocean(), hidden, first_grad)
    up_ref[0:cols, :] = hidden[cols:]
    up_ref[cols:, :] = first_grad[cols:]
    down_ref[0:cols, :] = hidden[:cols]
    down_ref[cols:, :] = first_grad[:cols]


def grad_atmos(pad, own, pad_is_input, cols, store):
    rows = own.shape[0]
    if pad_is_input:
        middle = pad.T
        before, after = moved_cells(middle, 1, cols)
        lefts = [part.astype(BF16) for part in (before, middle, after)]
        right = own.astype(BF16)
        for tap in range(9):
            start = cols * (tap // 3)
            store(tap, dot(lefts[tap % 3][:, start : start + rows], right))
    else:
        left = own.T.astype(BF16)
        before, after = moved_cells(pad, 0, cols)
        rights = [part.astype(BF16) for part in (after, pad, before)]
        for tap in range(9):
            start = cols * (2 - tap // 3)
            store(tap, dot(left, rights[tap % 3][start : start + rows]))


def grad_ocean(pad, own, pad_is_input, cols, store):
    rows, channels = own.shape
    narrow = channels // 2

    if pad_is_input:
        middle = pad.T
        before, after = moved_cells(middle, 1, cols)
        even, odd = middle[:narrow].astype(BF16), middle[narrow:].astype(BF16)
        pairs = (
            (before[narrow:].astype(BF16), even),
            (even, odd),
            (odd, after[:narrow].astype(BF16)),
        )
        right = jnp.concatenate(halves_apart(own, narrow), axis=0).astype(BF16)
        for tap in range(9):
            start = cols * (tap // 3)
            pieces = [part[:, start : start + rows] for part in pairs[tap % 3]]
            store(tap, dot(jnp.concatenate(pieces, axis=1), right))
    else:
        turned = own.T.astype(BF16)
        left = jnp.concatenate([turned[:narrow], turned[narrow:]], axis=1)
        even, odd = halves_apart(pad, narrow)
        odd_before = moved_cells(odd, 0, cols)[0].astype(BF16)
        even_after = moved_cells(even, 0, cols)[1].astype(BF16)
        even, odd = even.astype(BF16), odd.astype(BF16)
        pairs = ((odd, even_after), (even, odd), (odd_before, even))
        for tap in range(9):
            start = cols * (2 - tap // 3)
            pieces = [part[start : start + rows] for part in pairs[tap % 3]]
            store(tap, dot(left, jnp.concatenate(pieces, axis=0)))


def store_into(out_ref):
    def store(tap, value):
        if len(out_ref.shape) == 2:
            rows = value.shape[0]
            out_ref[rows * tap : rows * (tap + 1), :] = value
        else:
            rows = value.shape[0]
            for piece in range(out_ref.shape[0]):
                lanes = slice(128 * piece, 128 * (piece + 1))
                out_ref[piece, rows * tap : rows * (tap + 1), :] = value[:, lanes]

    return store


def own_grads_kernel(upad_ref, gpad_ref, stay_ref, atmos_out, ocean_out, *, cols):
    stay = stay_ref[...].astype(F32)

    @pl.when(on_ocean())
    def _():
        grad_ocean(upad_ref[...].astype(F32), stay, True, cols, store_into(ocean_out))

    @pl.when(jnp.logical_not(on_ocean()))
    def _():
        grad_atmos(gpad_ref[...].astype(F32), stay, False, cols, store_into(atmos_out))


def other_grads(early_ref, late_ref, sent_ref, coupling_ref, atmos_out, ocean_out, cols):
    late = late_ref[...].astype(F32)
    early = early_ref[...].astype(F32)

    @pl.when(on_ocean())
    def _():
        added = dot(sent_ref[...], coupling_ref[...].astype(F32), TN, HIGHEST)
        other = (early + added).astype(BF16).astype(F32)
        grad_atmos(other, late, True, cols, store_into(atmos_out))

    @pl.when(jnp.logical_not(on_ocean()))
    def _():
        grad_ocean(early, late, False, cols, store_into(ocean_out))


def chunk_rows(keep_ref, send_ref, atmos_all, ocean_all, chunks):
    channels = keep_ref.shape[2]
    pieces = ocean_all.shape[0]
    atmos_rows = atmos_all.shape[0] // chunks
    ocean_rows = atmos_rows // 2
    taken = keep_ref.shape[1] - atmos_rows
    core = lax.rem(lax.axis_index("lat"), 2)
    blank = jnp.zeros((taken, channels - 128 * pieces), F32)
    for out_ref, side in ((send_ref, 1 - core), (keep_ref, core)):
        for pair in range(chunks // 2):
            start = pl.multiple_of(atmos_rows * (2 * pair + side), 8)
            upper = atmos_all[pl.ds(start, atmos_rows), :]
            start = ocean_rows * (2 * pair + side)
            halves = []
            for odd in range(2):
                parts = [ocean_all.at[piece][pl.ds(start + odd, taken, 2), :] for piece in range(pieces)]
                halves.append(jnp.concatenate(parts + [blank], axis=1))
            lower = halves[0] + pltpu.roll(halves[1], channels // 2, 1)
            out_ref[pair] = jnp.concatenate([upper, lower], axis=0).astype(BF16)


def grads_kernel(
    early_ref, late_ref, sent_ref, coupling_ref, atmos_in, ocean_in,
    keep_ref, send_ref, atmos_all, ocean_all, *, cols, chunks,
):
    other_grads(early_ref, late_ref, sent_ref, coupling_ref, atmos_all, ocean_all, cols)

    @pl.when(on_ocean())
    def _():
        chunk_rows(keep_ref, send_ref, atmos_all, ocean_in, chunks)

    @pl.when(jnp.logical_not(on_ocean()))
    def _():
        chunk_rows(keep_ref, send_ref, atmos_in, ocean_all, chunks)


def plain_grads_kernel(
    early_ref, late_ref, sent_ref, coupling_ref, atmos_in, ocean_in, atmos_out, ocean_out, *, cols
):
    @pl.when(on_ocean())
    def _():
        ocean_out[...] = ocean_in[...]

    @pl.when(jnp.logical_not(on_ocean()))
    def _():
        atmos_out[...] = atmos_in[...]

    other_grads(early_ref, late_ref, sent_ref, coupling_ref, atmos_out, ocean_out, cols)


def own_bit(bit):
    return lax.rem(lax.shift_right_logical(lax.axis_index("lat"), bit), 2)


def halve(keep_ref, came_ref, keep_out, send_out, bit, rows):
    own = own_bit(bit)
    for out_ref, side in ((send_out, 1 - own), (keep_out, own)):
        for outer in range(keep_ref.shape[0]):
            for inner in range(keep_ref.shape[2]):
                total = keep_ref[outer, side, inner, rows, :].astype(F32)
                total = total + came_ref[outer, side, inner, rows, :].astype(F32)
                out_ref[outer, inner] = total.astype(BF16)


def split_kernel(keep_ref, came_ref, done_ref, first_keep, first_send, second_keep, second_send, *, cut):
    tall = keep_ref.shape[3]
    halve(keep_ref, came_ref, first_keep, first_send, 1, slice(0, cut))
    views = [ref.reshape(2, 2, 2, *keep_ref.shape[3:]) for ref in (keep_ref, came_ref)]
    halve(*views, second_keep, second_send, 2, slice(cut, tall))


def halve_kernel(keep_ref, came_ref, *refs, bit):
    keep_out, send_out = refs[-2:]
    halve(keep_ref, came_ref, keep_out, send_out, bit, slice(None))


def halved(keep, came, bit, dims, after=()):
    outer, inner, rows, channels = dims[0], dims[1], keep.shape[-2], keep.shape[-1]
    keep, came = (part.reshape(outer, 2, inner, rows, channels) for part in (keep, came))
    out = shape((outer, inner, rows, channels), BF16)
    return call(
        functools.partial(halve_kernel, bit=bit),
        [out, out],
        [keep, came, *after],
        [WHOLE] * 2 + [IN_PLACE] * len(after),
        moved=8 * outer * inner * rows * channels,
        name="halve",
    )


def scatter_sum(keep, came, done_before, done_next):
    pairs, tall, channels = keep.shape
    cut = -(-tall // 32) * 16
    first, second = shape((4, 1, cut, channels), BF16), shape((2, 2, tall - cut, channels), BF16)
    keep, came = (part.reshape(4, 2, 1, tall, channels) for part in (keep, came))
    first_keep, first_send, second_keep, second_send = call(
        functools.partial(split_kernel, cut=cut),
        [first, first, second, second],
        [keep, came, done_before],
        [WHOLE] * 2 + [ANYWHERE],
        moved=6 * pairs * tall * channels,
        name="split",
    )
    first_came = swapped(first_send, "lat", 2)
    second_came = swapped(second_send, "lat", 4)
    first_keep, first_send = halved(first_keep, first_came, 2, (2, 1), done_next)
    first_came = swapped(first_send, "lat", 4)
    second_keep, second_send = halved(second_keep, second_came, 3, (1, 2))
    second_came = swapped(second_send, "lat", 8)
    first_keep, first_send = halved(first_keep, first_came, 3, (1, 1))
    first_came = swapped(first_send, "lat", 8)
    second_keep, second_send = halved(second_keep, second_came, 1, (1, 1))
    second_came = swapped(second_send, "lat", 2)
    return [part.reshape(-1, channels) for part in (first_keep, first_came, second_keep, second_came)]


def finish_kernel(
    first_ref, first_came, second_ref, second_came, atmos_ref, ocean_ref, *, atmos_factor, ocean_factor
):
    channels = first_ref.shape[1]
    pieces = channels // 128
    atmos_rows = atmos_ref.shape[0] // pieces
    ocean_rows = ocean_ref.shape[0] // pieces
    first = first_ref[...].astype(F32) + first_came[...].astype(F32)
    second = second_ref[...].astype(F32) + second_came[...].astype(F32)
    total = jnp.concatenate([first, second], axis=0)
    for piece in range(pieces):
        lanes = slice(128 * piece, 128 * (piece + 1))
        atmos_ref[pl.ds(piece, atmos_rows, pieces), :] = total[:atmos_rows, lanes] * atmos_factor
        ocean_ref[pl.ds(piece, ocean_rows, pieces), :] = (
            total[atmos_rows : atmos_rows + ocean_rows, lanes] * ocean_factor
        )


def input_grad_kernel(
    stay_ref, give_ref, low_ref, high_ref, gpad_ref, wet_ref, terms_ref, atmos_ref, ocean_ref,
    grad_ref, sent_ref, pad_ref, *scratch, cols,
):
    def gather():
        pad_ref[0:cols, :] = low_ref[cols:, :]
        pad_ref[cols : 3 * cols, :] = jnp.where(on_ocean(), stay_ref[...], give_ref[...])
        pad_ref[3 * cols :, :] = high_ref[cols:, :]

    own = slice(cols, 3 * cols)
    convolve(pad_ref, grad_ref, atmos_ref, ocean_ref, 0, True, scratch, cols, gather)
    grad = gpad_ref[own, :].astype(F32) + grad_ref[...]
    grad_ref[...] = grad
    weighted = dot(terms_ref[8:16, :], grad, NT, HIGHEST)
    mixed = weighted[0:4] * wet_ref[0:1, own] + weighted[4:8] * wet_ref[1:2, own]
    sent_ref[...] = jnp.where(on_ocean(), mixed, weighted[0:4])


def next_kernel(
    stay_ref, give_ref, low_ref, high_ref, upad_ref, atmos_ref, ocean_ref,
    next_ref, mark_ref, second_ref, pad_ref, *scratch, cols,
):
    def gather():
        pad_ref[0:cols, :] = low_ref[0:cols, :]
        pad_ref[cols : 3 * cols, :] = jnp.where(on_ocean(), give_ref[...], stay_ref[...])
        pad_ref[3 * cols :, :] = high_ref[0:cols, :]

    own = slice(cols, 3 * cols)
    convolve(pad_ref, second_ref, atmos_ref, ocean_ref, 1, False, scratch, cols, gather)
    values = (upad_ref[own, :].astype(F32) + second_ref[...]).astype(BF16)
    next_ref[0] = values[:cols]
    next_ref[1] = values[cols:]
    mark_ref[...] = jnp.zeros_like(mark_ref)


def last_kernel(grad_ref, arrived_ref, wet_ref, terms_ref, out_ref, mark_ref, *, cols):
    own = slice(cols, 3 * cols)
    wet = wet_ref[0:1, own], wet_ref[1:2, own]
    arrived = jnp.where(on_ocean(), arrived_ref[...] * wet_ref[2:3, own], arrived_ref[...])
    added = spread(arrived, wet, on_ocean(), terms_ref[0:8, :])
    values = (grad_ref[...] + added).astype(BF16)
    out_ref[0] = values[:cols]
    out_ref[1] = values[cols:]
    mark_ref[...] = jnp.zeros_like(mark_ref)


def swapped(value, axis, mask):
    pairs = [(source, source ^ mask) for source in range(lax.axis_size(axis))]
    return lax.ppermute(value, axis, pairs)


def halo(up, down):
    count = lax.axis_size("lat")
    forward = [(i, i + 1) for i in range(count - 1)]
    backward = [(target, source) for source, target in forward]
    return lax.ppermute(up, "lat", forward), lax.ppermute(down, "lat", backward)


def local(
    fields,
    cotangent,
    ocean_kernels,
    atmos_kernels,
    ocean_surface,
    ocean_coupling,
    atmos_flux,
    atmos_coupling,
    row_map,
    wet_mask,
):
    x, g = fields[0], cotangent[0]
    bands, cols, channels = x.shape
    narrow = channels // 2
    cells = bands * cols
    count = lax.axis_size("lat")
    is_ocean = lax.axis_index("grp") == 0
    atmos_factor = 1.0 / math.sqrt(bands * count * cols)
    ocean_factor = 1.0 / math.sqrt(bands * count * 2 * cols)
    bound = functools.partial

    blank = jnp.zeros((4, narrow), BF16)
    gap = jnp.zeros((4, channels), BF16)
    surface = ocean_surface.T
    ocean_terms = jnp.concatenate(
        [
            jnp.concatenate([surface, blank], axis=1),
            jnp.concatenate([blank, surface], axis=1),
            jnp.concatenate([ocean_coupling, blank], axis=1),
            jnp.concatenate([blank, ocean_coupling], axis=1),
        ],
        axis=0,
    )
    atmos_terms = jnp.concatenate([atmos_flux.T, gap, atmos_coupling, gap], axis=0)
    terms = jnp.where(is_ocean, ocean_terms, atmos_terms).astype(F32)

    edge = shape((2 * cols + 16, channels), BF16)
    kept = shape(x.shape, BF16)
    up, down = call(
        bound(pack_kernel, cols=cols),
        [edge, edge],
        [x, g, wet_mask],
        [IN_PLACE] * 3,
        [
            pltpu.VMEM(wet_mask.shape, jnp.int32),
            pltpu.VMEM((2, 16, channels), BF16),
            pltpu.SemaphoreType.DMA,
            pltpu.SemaphoreType.DMA((2, 3)),
        ],
        out_spec=ANYWHERE,
        name="pack",
        limit=PACK_VMEM,
    )
    low, high = halo(up, down)
    x, g, own_wet = call(
        bound(hold_kernel, cols=cols),
        [kept, kept, shape((16, channels), BF16)],
        [x, g, wet_mask],
        [IN_PLACE] * 3,
        [pltpu.VMEM(wet_mask.shape, jnp.int32), pltpu.SemaphoreType.DMA((3,))],
        flops=PACE * 10**8,
        name="hold",
        limit=MOST_VMEM,
    )
    atmos_flat = atmos_kernels.reshape(18, channels, channels)
    ocean_flat = ocean_kernels.reshape(18, narrow, narrow)
    pad = shape((2 * cells, channels), BF16)
    xpad, gpad, wet, early, sent = call(
        bound(outgoing_kernel, cols=cols),
        [pad, pad, shape((8, 2 * cells), F32), pad, shape((4, 2 * cells), F32)],
        [x, g, low, high, own_wet, terms],
        name="outgoing",
    )
    arrived = swapped(sent, "grp", 1)
    other_early = swapped(early, "grp", 1)
    conv_cost = dict(limit=MOST_VMEM, flops=PACE * 9 * cells * channels * channels, moved=9 * channels * channels * 2)
    grad_cost = dict(conv_cost, limit=VMEM_LIMIT)
    back = call(
        bound(back_kernel, cols=cols),
        shape((cells, channels), F32),
        [gpad, atmos_flat, ocean_flat],
        [WHOLE, IN_PLACE, IN_PLACE],
        conv_scratch(channels),
        **conv_cost,
        name="back",
    )
    half = shape((cells, channels), BF16)
    upad, stay, give, up, down = call(
        bound(first_kernel, cols=cols),
        [pad, half, half, half, half],
        [xpad, wet, arrived, terms, back, atmos_flat, ocean_flat],
        [WHOLE] * 5 + [IN_PLACE] * 2,
        [pltpu.VMEM((cells, channels), F32)] + conv_scratch(channels),
        **conv_cost,
        name="first",
    )
    late = swapped(give, "grp", 1)

    atmos_rows = 9 * channels // count
    ocean_rows = 9 * narrow // count
    wide = -(-narrow // 128) * 128
    chunked = count == 16 and 9 * channels % (8 * count) == 0 and ocean_rows % 2 == 0
    tall = -(-(atmos_rows + ocean_rows // 2) // 16) * 16
    spare = max(0, 2 * (tall - atmos_rows) - ocean_rows) if chunked else 0
    ocean_tall = 9 * narrow + -(-spare // 8) * 8
    sums = [shape((9 * channels, channels), F32), shape((wide // 128, ocean_tall, 128), F32)]
    atmos_sum, ocean_sum = call(
        bound(own_grads_kernel, cols=cols), sums, [upad, gpad, stay], **grad_cost, name="own_grads"
    )
    inputs = [other_early, late, sent, atmos_coupling, atmos_sum, ocean_sum]
    if chunked:
        part = shape((count // 2, tall, channels), BF16)
        keep, send = call(
            bound(grads_kernel, cols=cols, chunks=count),
            [part, part],
            inputs,
            None,
            [pltpu.VMEM(out.shape, F32) for out in sums],
            **grad_cost,
            name="grads",
        )
        came = swapped(send, "lat", 1)
    else:
        atmos_all, ocean_all = call(
            bound(plain_grads_kernel, cols=cols), sums, inputs, **grad_cost, name="grads"
        )

    low, high = halo(up, down)
    grad, sent_back = call(
        bound(input_grad_kernel, cols=cols),
        [shape((cells, channels), F32), shape((4, cells), F32)],
        [stay, give, low, high, gpad, wet, terms, atmos_flat, ocean_flat],
        [WHOLE] * 7 + [IN_PLACE] * 2,
        [pltpu.VMEM((2 * cells, channels), BF16)] + conv_scratch(channels),
        **conv_cost,
        name="input_grad",
    )
    returned = swapped(sent_back, "grp", 1)
    mark = shape((8, 128), F32)
    next_field, next_mark = call(
        bound(next_kernel, cols=cols),
        [shape(x.shape, BF16), mark],
        [stay, give, low, high, upad, atmos_flat, ocean_flat],
        [WHOLE] * 5 + [IN_PLACE] * 2,
        [pltpu.VMEM((cells, channels), F32), pltpu.VMEM((2 * cells, channels), BF16)] + conv_scratch(channels),
        **conv_cost,
        name="next",
    )
    field_grad, last_mark = call(
        bound(last_kernel, cols=cols),
        [shape(x.shape, BF16), mark],
        [grad, returned, wet, terms],
        name="last",
    )

    if chunked:
        atmos_chunk, ocean_chunk = call(
            bound(finish_kernel, atmos_factor=atmos_factor, ocean_factor=ocean_factor),
            [
                shape((atmos_rows * channels // 128, 128), F32),
                shape((ocean_rows * narrow // 128, 128), F32),
            ],
            scatter_sum(keep, came, sent_back, (next_mark, last_mark)),
            name="finish",
        )
        atmos_total, ocean_total = atmos_chunk.reshape(-1), ocean_chunk.reshape(-1)
    else:
        atmos_total = atmos_factor * lax.psum_scatter(
            atmos_all.reshape(-1), "lat", scatter_dimension=0, tiled=True
        )
        ocean_all = jnp.concatenate([ocean_all[piece] for piece in range(wide // 128)], axis=1)
        ocean_total = ocean_factor * lax.psum_scatter(
            ocean_all[:, :narrow].reshape(-1), "lat", scatter_dimension=0, tiled=True
        )
    return (next_field[None], field_grad[None], ocean_total, atmos_total)


def solution(mesh):
    in_specs = (
        P("grp", "lat", None, None),
        P("grp", "lat", None, None),
        P(),
        P(),
        P(),
        P(),
        P(),
        P(),
        P("lat"),
        P("lat", None),
    )
    out_specs = (
        P("grp", "lat", None, None),
        P("grp", "lat", None, None),
        P(("grp", "lat")),
        P(("grp", "lat")),
    )
    return jax.shard_map(local, mesh=mesh, in_specs=in_specs, out_specs=out_specs, check_vma=False)
```

time: 91.2 us -> 92.4 us (1.013)
  Pallas kernels: 26.3 us -> 32.4 us
  local copies, waits for them, and re-layouts: 7.06 us -> 2.55 us
  waiting for transfers between devices: 27.1 us -> 28.4 us
  starting transfers between devices: 28.6 us -> 27.4 us
    pallas_call x14 -> x16, Pallas kernels: 26.3 us -> 32.4 us  [call(): pl.pallas_call(kernel, out_shape=outs, in_specs=in_specs or [WHOLE] * len...]
    unnamed x16 -> x14, local copies, waits for them, and re-layouts: 7.06 us -> 2.55 us
    ppermute x2, waiting for transfers between devices: 3.3 us -> 6.51 us  [halo(): lax.ppermute(down, 'lat', backward)]
    ppermute x11, waiting for transfers between devices: 23.8 us -> 21.7 us  [swapped(): return lax.ppermute(value, axis, pairs)]
    ppermute x11, starting transfers between devices: 22.2 us -> 20.5 us  [swapped(): return lax.ppermute(value, axis, pairs)]
  transfers between devices with their start and end apart: 15 -> 15, of which waited for: 7 -> 9; matrix products, arithmetic and copies ran while one was open for 1% -> 0% of each run, Pallas kernels for 21% -> 16%
where the time goes in v1:
time: 92.4 us; the launch traced here: 91.7 us
  Pallas kernels  32.4 us (35%)
  waiting for transfers between devices  28.4 us (31%)
  starting transfers between devices  27.4 us (30%)
  local copies, waits for them, and re-layouts  2.55 us (3%)
    pallas_call x16, Pallas kernels, call(): pl.pallas_call(kernel, out_shape=outs, in_specs=in_specs or [WHOLE] * len...  32.4 us
    ppermute x11, waiting for transfers between devices, swapped(): return lax.ppermute(value, axis, pairs)  21.7 us
    ppermute x11, starting transfers between devices, swapped(): return lax.ppermute(value, axis, pairs)  20.5 us
    ppermute x2, waiting for transfers between devices, halo(): lax.ppermute(down, 'lat', backward)  6.51 us
    ppermute x2, starting transfers between devices, halo(): lax.ppermute(up, 'lat', forward)  4.3 us
    ppermute x2, starting transfers between devices, halo(): lax.ppermute(down, 'lat', backward)  2.58 us
    unnamed x14, local copies, waits for them, and re-layouts  2.55 us
  transfers between devices with their start and end apart: 15, of which 9 were waited for; matrix products, arithmetic and copies ran while one was open for 0% of the time, Pallas kernels for 16%

profile of v1, /device:TPU:0, one launch (start us, length us, event | category | flops | bytes accessed | tf_op | source)
XLA Modules:
  0.0 91.7 jit_solution(11388429526118726841)
XLA Ops:
  0.7 13.1 %pack.1 = (bf16[272,384]{1,0:T(8,128)(2,1)}, bf16[272,384]{1,0:T(8,128)(2,1)}) custom-call(bf16[2,128,384]{2,1,0:T(8,128)(2,1)} %bitcast.33, bf16[2,128,384]{2,1,0:T(8,128)(2,1)} %bitcast.35, s32[2,256]{1,0:T(2,128)} %wet_any.3), custom_call_target="tpu_custom_call" | custom-call | tf_op jit(solution)/shard_map/pack/pallas_call | solution.py:34
  13.8 2.4 %collective-permute-start = (bf16[272,384]{1,0:T(8,128)(2,1)}, bf16[272,384]{1,0:T(8,128)(2,1)S(1)}, u32[]{:S(2)}, u32[]{:S(2)}) collective-permute-start(bf16[272,384]{1,0:T(8,128)(2,1)} %get-tuple-element.45), channel_id=1, source_target_pairs={{0,1},{1,2},{2,3},{3,4},{4,5},{5,6},{6,7},{7,8},{8,9},{9,10},{10,1... | collective-permute-start | bytes 626696 | tf_op jit(solution)/shard_map/ppermute | solution.py:552
  16.1 1.3 %collective-permute-start.1 = (bf16[272,384]{1,0:T(8,128)(2,1)}, bf16[272,384]{1,0:T(8,128)(2,1)S(1)}, u32[]{:S(2)}, u32[]{:S(2)}) collective-permute-start(bf16[272,384]{1,0:T(8,128)(2,1)} %get-tuple-element.46), channel_id=1, source_target_pairs={{1,0},{2,1},{3,2},{4,3},{5,4},{6,5},{7,6},{8,7},{9,8},{10,9},{11,1... | collective-permute-start | bytes 626696 | tf_op jit(solution)/shard_map/ppermute | solution.py:552
  17.5 0.9 %copy-done = bf16[1,2,128,384]{3,2,1,0:T(8,128)(2,1)S(1)} copy-done((bf16[1,2,128,384]{3,2,1,0:T(8,128)(2,1)S(1)}, bf16[1,2,128,384]{3,2,1,0:T(8,128)(2,1)}, u32[]{:S(2)}) %copy-start) | copy-done | bytes 196632
  18.4 0.9 %copy-done.1 = bf16[1,2,128,384]{3,2,1,0:T(8,128)(2,1)S(1)} copy-done((bf16[1,2,128,384]{3,2,1,0:T(8,128)(2,1)S(1)}, bf16[1,2,128,384]{3,2,1,0:T(8,128)(2,1)}, u32[]{:S(2)}) %copy-start.1) | copy-done | bytes 196632
  19.3 0.7 copy-done.3
  20.0 0.7 hold.1
  20.8 1.0 %collective-permute-done.1.high_ref = bf16[272,384]{1,0:T(8,128)(2,1)S(1)} collective-permute-done((bf16[272,384]{1,0:T(8,128)(2,1)}, bf16[272,384]{1,0:T(8,128)(2,1)S(1)}, u32[]{:S(2)}, u32[]{:S(2)}) %collective-permute-start.1) | collective-permute-done | bytes 208928 | tf_op jit(solution)/shard_map/ppermute | solution.py:552
  22.1 1.5 %collective-permute-start.2 = (f32[4,512]{1,0:T(4,128)S(1)}, f32[4,512]{1,0:T(4,128)S(1)}, u32[]{:S(2)}, u32[]{:S(2)}) collective-permute-start(f32[4,512]{1,0:T(4,128)S(1)} %get-tuple-element.50.sent_ref), channel_id=1, source_target_pairs={{0,16},{16,0},{1,17},{17,1},{2,18},{18,2},{3,19},{19,3},{4,20},{20... | collective-permute-start | bytes 24584 | tf_op jit(solution)/shard_map/ppermute | solution.py:545
  23.7 0.5 collective-permute-start.6
  24.2 2.5 %back.1.back_ref = f32[256,384]{1,0:T(8,128)S(1)} custom-call(bf16[512,384]{1,0:T(8,128)(2,1)S(1)} %get-tuple-element.51.gpad_ref, bf16[18,384,384]{2,1,0:T(8,128)(2,1)} %bitcast.46, bf16[18,192,192]{2,1,0:T(8,128)(2,1)} %bitcast.50), custom_call_target="tpu_custom_call" | custom-call | flops 2717908992 | bytes 2654208 | tf_op jit(solution)/shard_map/back/pallas_call | solution.py:34
  26.7 2.8 %first.1 = (bf16[512,384]{1,0:T(8,128)(2,1)S(1)}, bf16[256,384]{1,0:T(8,128)(2,1)S(1)}, bf16[256,384]{1,0:T(8,128)(2,1)S(1)}, bf16[256,384]{1,0:T(8,128)(2,1)S(1)}, bf16[256,384]{1,0:T(8,128)(2,1)S(1)}) custom-call(bf16[512,384]{1,0:T(8,128)(2,1)S(1)} %get-tuple-element.48.xpad_ref, f32[8,512]{1,0:T(8,128)S(1)} %get-tuple-element.49.wet_ref, ...), custom_call_target="tpu_custom_call" | custom-call | flops 2717908992 | bytes 2654208 | tf_op jit(solution)/shard_map/first/pallas_call | solution.py:34
  29.4 2.6 %collective-permute-start.7 = (bf16[256,384]{1,0:T(8,128)(2,1)S(1)}, bf16[256,384]{1,0:T(8,128)(2,1)S(1)}, u32[]{:S(2)}, u32[]{:S(2)}) collective-permute-start(bf16[256,384]{1,0:T(8,128)(2,1)S(1)} %get-tuple-element.53.give_ref), channel_id=1, source_target_pairs={{0,16},{16,0},{1,17},{17,1},{2,18},{18,2},{3,19},{19,3},{4,20},{20... | collective-permute-start | bytes 589832 | tf_op jit(solution)/shard_map/ppermute | solution.py:545
  32.0 0.9 %own_grads.1 = (f32[3456,384]{1,0:T(8,128)S(1)}, f32[2,1736,128]{2,1,0:T(8,128)S(1)}) custom-call(bf16[512,384]{1,0:T(8,128)(2,1)S(1)} %get-tuple-element.56.upad_ref, bf16[512,384]{1,0:T(8,128)(2,1)S(1)} %get-tuple-element.51.gpad_ref, bf16[256,384]{1,0:T(8,128)(2,1)S(1)} %get-tuple-element.52.stay_ref), custom_call_target="tpu_custom_call" | custom-call | flops 2717908992 | bytes 2654208 | tf_op jit(solution)/shard_map/own_grads/pallas_call | solution.py:34
  33.0 4.9 %collective-permute-done.7.late_ref = bf16[256,384]{1,0:T(8,128)(2,1)S(1)} collective-permute-done((bf16[256,384]{1,0:T(8,128)(2,1)S(1)}, bf16[256,384]{1,0:T(8,128)(2,1)S(1)}, u32[]{:S(2)}, u32[]{:S(2)}) %collective-permute-start.7) | collective-permute-done | bytes 196640 | tf_op jit(solution)/shard_map/ppermute | solution.py:545
  37.8 3.3 %grads.1 = (bf16[8,272,384]{2,1,0:T(8,128)(2,1)S(1)}, bf16[8,272,384]{2,1,0:T(8,128)(2,1)S(1)}) custom-call(bf16[512,384]{1,0:T(8,128)(2,1)S(1)} %collective-permute-done.6.early_ref, bf16[256,384]{1,0:T(8,128)(2,1)S(1)} %collective-permute-done.7.late_ref, f32[4,512]{1,0:T(4,128)S(1)} %get-tuple-element.50.sent_ref, bf16[4,384]{1,0:T(4,128)(2,1)S(1)} %copy-done.2, ...), custom_call_target="tpu_custom_call" | custom-call | flops 2717908992 | bytes 2654208 | tf_op jit(solution)/shard_map/grads/pallas_call | solution.py:34
  41.2 2.0 %collective-permute-start.8 = (bf16[8,272,384]{2,1,0:T(8,128)(2,1)S(1)}, bf16[8,272,384]{2,1,0:T(8,128)(2,1)S(1)}, u32[]{:S(2)}, u32[]{:S(2)}) collective-permute-start(bf16[8,272,384]{2,1,0:T(8,128)(2,1)S(1)} %get-tuple-element.65), channel_id=1, source_target_pairs={{0,1},{1,0},{2,3},{3,2},{4,5},{5,4},{6,7},{7,6},{8,9},{9,8},{10,11... | collective-permute-start | bytes 5013512 | tf_op jit(solution)/shard_map/ppermute | solution.py:545
  43.2 1.9 %collective-permute-start.3 = (bf16[256,384]{1,0:T(8,128)(2,1)S(1)}, bf16[256,384]{1,0:T(8,128)(2,1)S(1)}, u32[]{:S(2)}, u32[]{:S(2)}) collective-permute-start(bf16[256,384]{1,0:T(8,128)(2,1)S(1)} %get-tuple-element.54), channel_id=1, source_target_pairs={{0,1},{1,2},{2,3},{3,4},{4,5},{5,6},{6,7},{7,8},{8,9},{9,10},{10,1... | collective-permute-start | bytes 589832 | tf_op jit(solution)/shard_map/ppermute | solution.py:552
  45.1 1.3 %collective-permute-start.4 = (bf16[256,384]{1,0:T(8,128)(2,1)S(1)}, bf16[256,384]{1,0:T(8,128)(2,1)S(1)}, u32[]{:S(2)}, u32[]{:S(2)}) collective-permute-start(bf16[256,384]{1,0:T(8,128)(2,1)S(1)} %get-tuple-element.55), channel_id=1, source_target_pairs={{1,0},{2,1},{3,2},{4,3},{5,4},{6,5},{7,6},{8,7},{9,8},{10,9},{11,1... | collective-permute-start | bytes 589832 | tf_op jit(solution)/shard_map/ppermute | solution.py:552
  46.6 5.5 %collective-permute-done.4.high_ref = bf16[256,384]{1,0:T(8,128)(2,1)S(1)} collective-permute-done((bf16[256,384]{1,0:T(8,128)(2,1)S(1)}, bf16[256,384]{1,0:T(8,128)(2,1)S(1)}, u32[]{:S(2)}, u32[]{:S(2)}) %collective-permute-start.4) | collective-permute-done | bytes 196640 | tf_op jit(solution)/shard_map/ppermute | solution.py:552
  52.1 2.9 %input_grad.1 = (f32[256,384]{1,0:T(8,128)S(1)}, f32[4,256]{1,0:T(4,128)S(1)}) custom-call(bf16[256,384]{1,0:T(8,128)(2,1)S(1)} %get-tuple-element.52.stay_ref, bf16[256,384]{1,0:T(8,128)(2,1)S(1)} %get-tuple-element.53.give_ref, bf16[256,384]{1,0:T(8,128)(2,1)S(1)} %collective-permute-done.3.low_ref, bf16[256,384]{1,0:T(8,128)(2,1)S(1)} %collective-permute-done.4.high_ref, ...), custom_call_target="tpu_custom_call" | custom-call | flops 2717908992 | bytes 2654208 | tf_op jit(solution)/shard_map/input_grad/pallas_call | solution.py:34
  55.5 3.9 %collective-permute-start.9 = (bf16[4,1,144,384]{3,2,1,0:T(8,128)(2,1)S(1)}, bf16[4,1,144,384]{3,2,1,0:T(8,128)(2,1)S(1)}, u32[]{:S(2)}, u32[]{:S(2)}) collective-permute-start(bf16[4,1,144,384]{3,2,1,0:T(8,128)(2,1)S(1)} %get-tuple-element.67), channel_id=1, source_target_pairs={{0,2},{1,3},{2,0},{3,1},{4,6},{5,7},{6,4},{7,5},{8,10},{9,11},{10,... | collective-permute-start | bytes 1327112 | tf_op jit(solution)/shard_map/ppermute | solution.py:545
  59.4 1.6 %collective-permute-start.12 = (bf16[2,2,128,384]{3,2,1,0:T(8,128)(2,1)S(1)}, bf16[2,2,128,384]{3,2,1,0:T(8,128)(2,1)S(1)}, u32[]{:S(2)}, u32[]{:S(2)}) collective-permute-start(bf16[2,2,128,384]{3,2,1,0:T(8,128)(2,1)S(1)} %get-tuple-element.75), channel_id=1, source_target_pairs={{0,4},{1,5},{2,6},{3,7},{4,0},{5,1},{6,2},{7,3},{8,12},{9,13},{10,... | collective-permute-start | bytes 1179656 | tf_op jit(solution)/shard_map/ppermute | solution.py:545
  61.0 3.2 %next.1 = (bf16[2,128,384]{2,1,0:T(8,128)(2,1)}, f32[8,128]{1,0:T(8,128)S(1)}) custom-call(bf16[256,384]{1,0:T(8,128)(2,1)S(1)} %get-tuple-element.52.stay_ref, bf16[256,384]{1,0:T(8,128)(2,1)S(1)} %get-tuple-element.53.give_ref, bf16[256,384]{1,0:T(8,128)(2,1)S(1)} %collective-permute-done.3.low_ref, bf16[256,384]{1,0:T(8,128)(2,1)S(1)} %collective-permute-done.4.high_ref, ...), custom_call_target="tpu_custom_call" | custom-call | flops 2717908992 | bytes 2654208 | tf_op jit(solution)/shard_map/next/pallas_call | solution.py:34
  64.6 1.2 %last.1 = (bf16[2,128,384]{2,1,0:T(8,128)(2,1)}, f32[8,128]{1,0:T(8,128)S(1)}) custom-call(f32[256,384]{1,0:T(8,128)S(1)} %get-tuple-element.58.grad_ref, f32[4,256]{1,0:T(4,128)S(1)} %collective-permute-done.5.arrived_ref, f32[8,512]{1,0:T(8,128)S(1)} %get-tuple-element.49.wet_ref, f32[16,384]{1,0:T(8,128)S(1)} %fusion.9.terms_ref), custom_call_target="tpu_custom_call" | custom-call | tf_op jit(solution)/shard_map/last/pallas_call | solution.py:34
  65.8 2.0 %collective-permute-done.9 = bf16[4,1,144,384]{3,2,1,0:T(8,128)(2,1)S(1)} collective-permute-done((bf16[4,1,144,384]{3,2,1,0:T(8,128)(2,1)S(1)}, bf16[4,1,144,384]{3,2,1,0:T(8,128)(2,1)S(1)}, u32[]{:S(2)}, u32[]{:S(2)}) %collective-permute-start.9) | collective-permute-done | bytes 442400 | tf_op jit(solution)/shard_map/ppermute | solution.py:545
  67.9 5.7 %collective-permute-start.10 = (bf16[2,1,144,384]{3,2,0,1:T(8,128)(2,1)S(1)}, bf16[2,1,144,384]{3,2,0,1:T(8,128)(2,1)S(1)}, u32[]{:S(2)}, u32[]{:S(2)}) collective-permute-start(bf16[2,1,144,384]{3,2,0,1:T(8,128)(2,1)S(1)} %bitcast.43), channel_id=1, source_target_pairs={{0,4},{1,5},{2,6},{3,7},{4,0},{5,1},{6,2},{7,3},{8,12},{9,13},{10,... | collective-permute-start | bytes 663560 | tf_op jit(solution)/shard_map/ppermute | solution.py:545
  73.7 2.4 %collective-permute-start.13 = (bf16[1,2,128,384]{3,2,1,0:T(8,128)(2,1)S(1)}, bf16[1,2,128,384]{3,2,1,0:T(8,128)(2,1)S(1)}, u32[]{:S(2)}, u32[]{:S(2)}) collective-permute-start(bf16[1,2,128,384]{3,2,1,0:T(8,128)(2,1)S(1)} %get-tuple-element.77), channel_id=1, source_target_pairs={{0,8},{1,9},{2,10},{3,11},{4,12},{5,13},{6,14},{7,15},{8,0},{9,1},... | collective-permute-start | bytes 589832 | tf_op jit(solution)/shard_map/ppermute | solution.py:545
  76.1 7.7 %collective-permute-done.10 = bf16[2,1,144,384]{3,2,0,1:T(8,128)(2,1)S(1)} collective-permute-done((bf16[2,1,144,384]{3,2,0,1:T(8,128)(2,1)S(1)}, bf16[2,1,144,384]{3,2,0,1:T(8,128)(2,1)S(1)}, u32[]{:S(2)}, u32[]{:S(2)}) %collective-permute-start.10) | collective-permute-done | bytes 221216 | tf_op jit(solution)/shard_map/ppermute | solution.py:545
  84.1 4.6 %collective-permute-done.14 = bf16[1,1,128,384]{3,2,1,0:T(8,128)(2,1)S(1)} collective-permute-done((bf16[1,1,128,384]{3,2,1,0:T(8,128)(2,1)S(1)}, bf16[1,1,128,384]{3,2,1,0:T(8,128)(2,1)S(1)}, u32[]{:S(2)}, u32[]{:S(2)}) %collective-permute-start.14) | collective-permute-done | bytes 98336 | tf_op jit(solution)/shard_map/ppermute | solution.py:545
  88.7 2.2 %collective-permute-done.11 = bf16[1,1,144,384]{3,2,1,0:T(8,128)(2,1)S(1)} collective-permute-done((bf16[1,1,144,384]{3,2,1,0:T(8,128)(2,1)S(1)}, bf16[1,1,144,384]{3,2,1,0:T(8,128)(2,1)S(1)}, u32[]{:S(2)}, u32[]{:S(2)}) %collective-permute-start.11) | collective-permute-done | bytes 110624 | tf_op jit(solution)/shard_map/ppermute | solution.py:545
  90.9 0.8 finish.1
  (30 shorter events, 2.0 us)
Async XLA Ops:
  0.6 20.0 %copy-start.2 = (bf16[4,384]{1,0:T(4,128)(2,1)S(1)}, bf16[4,384]{1,0:T(4,128)(2,1)}, u32[]{:S(2)}) copy-start(bf16[4,384]{1,0:T(4,128)(2,1)} %coupling_ref.1) | copy-start | bytes 9220
  0.6 20.0 %copy-start.4 = (bf16[384,4]{0,1:T(4,128)(2,1)S(1)}, bf16[384,4]{0,1:T(4,128)(2,1)}, u32[]{:S(2)}) copy-start(bf16[384,4]{0,1:T(4,128)(2,1)} %param.16) | copy-start | bytes 9220
  0.7 20.0 %copy-start.5 = (bf16[4,192]{1,0:T(4,128)(2,1)S(1)}, bf16[4,192]{1,0:T(4,128)(2,1)}, u32[]{:S(2)}) copy-start(bf16[4,192]{1,0:T(4,128)(2,1)} %param.15) | copy-start | bytes 4612
  0.7 20.0 %copy-start.6 = (bf16[192,4]{0,1:T(4,128)(2,1)S(1)}, bf16[192,4]{0,1:T(4,128)(2,1)}, u32[]{:S(2)}) copy-start(bf16[192,4]{0,1:T(4,128)(2,1)} %param.14) | copy-start | bytes 4612
  13.8 7.0 %collective-permute-start = (bf16[272,384]{1,0:T(8,128)(2,1)}, bf16[272,384]{1,0:T(8,128)(2,1)S(1)}, u32[]{:S(2)}, u32[]{:S(2)}) collective-permute-start(bf16[272,384]{1,0:T(8,128)(2,1)} %get-tuple-element.45), channel_id=1, source_target_pairs={{0,1},{1,2},{2,3},{3,4},{4,5},{5,6},{6,7},{7,8},{8,9},{9,10},{10,1... | collective-permute-start | bytes 626696 | tf_op jit(solution)/shard_map/ppermute | solution.py:552
  16.1 5.7 %collective-permute-start.1 = (bf16[272,384]{1,0:T(8,128)(2,1)}, bf16[272,384]{1,0:T(8,128)(2,1)S(1)}, u32[]{:S(2)}, u32[]{:S(2)}) collective-permute-start(bf16[272,384]{1,0:T(8,128)(2,1)} %get-tuple-element.46), channel_id=1, source_target_pairs={{1,0},{2,1},{3,2},{4,3},{5,4},{6,5},{7,6},{8,7},{9,8},{10,9},{11,1... | collective-permute-start | bytes 626696 | tf_op jit(solution)/shard_map/ppermute | solution.py:552
  17.4 0.9 %copy-start = (bf16[1,2,128,384]{3,2,1,0:T(8,128)(2,1)S(1)}, bf16[1,2,128,384]{3,2,1,0:T(8,128)(2,1)}, u32[]{:S(2)}) copy-start(bf16[1,2,128,384]{3,2,1,0:T(8,128)(2,1)} %param.10) | copy-start | bytes 589828
  18.4 0.9 %copy-start.1 = (bf16[1,2,128,384]{3,2,1,0:T(8,128)(2,1)S(1)}, bf16[1,2,128,384]{3,2,1,0:T(8,128)(2,1)}, u32[]{:S(2)}) copy-start(bf16[1,2,128,384]{3,2,1,0:T(8,128)(2,1)} %param.11) | copy-start | bytes 589828
  19.3 0.7 copy-start.3
  22.1 4.5 %collective-permute-start.2 = (f32[4,512]{1,0:T(4,128)S(1)}, f32[4,512]{1,0:T(4,128)S(1)}, u32[]{:S(2)}, u32[]{:S(2)}) collective-permute-start(f32[4,512]{1,0:T(4,128)S(1)} %get-tuple-element.50.sent_ref), channel_id=1, source_target_pairs={{0,16},{16,0},{1,17},{17,1},{2,18},{18,2},{3,19},{19,3},{4,20},{20... | collective-permute-start | bytes 24584 | tf_op jit(solution)/shard_map/ppermute | solution.py:545
  23.7 14.2 %collective-permute-start.6 = (bf16[512,384]{1,0:T(8,128)(2,1)S(1)}, bf16[512,384]{1,0:T(8,128)(2,1)S(1)}, u32[]{:S(2)}, u32[]{:S(2)}) collective-permute-start(bf16[512,384]{1,0:T(8,128)(2,1)S(1)} %get-tuple-element.61), channel_id=1, source_target_pairs={{0,16},{16,0},{1,17},{17,1},{2,18},{18,2},{3,19},{19,3},{4,20},{20... | collective-permute-start | bytes 1179656 | tf_op jit(solution)/shard_map/ppermute | solution.py:545
  29.4 8.4 %collective-permute-start.7 = (bf16[256,384]{1,0:T(8,128)(2,1)S(1)}, bf16[256,384]{1,0:T(8,128)(2,1)S(1)}, u32[]{:S(2)}, u32[]{:S(2)}) collective-permute-start(bf16[256,384]{1,0:T(8,128)(2,1)S(1)} %get-tuple-element.53.give_ref), channel_id=1, source_target_pairs={{0,16},{16,0},{1,17},{17,1},{2,18},{18,2},{3,19},{19,3},{4,20},{20... | collective-permute-start | bytes 589832 | tf_op jit(solution)/shard_map/ppermute | solution.py:545
  41.2 13.9 %collective-permute-start.8 = (bf16[8,272,384]{2,1,0:T(8,128)(2,1)S(1)}, bf16[8,272,384]{2,1,0:T(8,128)(2,1)S(1)}, u32[]{:S(2)}, u32[]{:S(2)}) collective-permute-start(bf16[8,272,384]{2,1,0:T(8,128)(2,1)S(1)} %get-tuple-element.65), channel_id=1, source_target_pairs={{0,1},{1,0},{2,3},{3,2},{4,5},{5,4},{6,7},{7,6},{8,9},{9,8},{10,11... | collective-permute-start | bytes 5013512 | tf_op jit(solution)/shard_map/ppermute | solution.py:545
  43.2 3.5 %collective-permute-start.3 = (bf16[256,384]{1,0:T(8,128)(2,1)S(1)}, bf16[256,384]{1,0:T(8,128)(2,1)S(1)}, u32[]{:S(2)}, u32[]{:S(2)}) collective-permute-start(bf16[256,384]{1,0:T(8,128)(2,1)S(1)} %get-tuple-element.54), channel_id=1, source_target_pairs={{0,1},{1,2},{2,3},{3,4},{4,5},{5,6},{6,7},{7,8},{8,9},{9,10},{10,1... | collective-permute-start | bytes 589832 | tf_op jit(solution)/shard_map/ppermute | solution.py:552
  45.1 7.0 %collective-permute-start.4 = (bf16[256,384]{1,0:T(8,128)(2,1)S(1)}, bf16[256,384]{1,0:T(8,128)(2,1)S(1)}, u32[]{:S(2)}, u32[]{:S(2)}) collective-permute-start(bf16[256,384]{1,0:T(8,128)(2,1)S(1)} %get-tuple-element.55), channel_id=1, source_target_pairs={{1,0},{2,1},{3,2},{4,3},{5,4},{6,5},{7,6},{8,7},{9,8},{10,9},{11,1... | collective-permute-start | bytes 589832 | tf_op jit(solution)/shard_map/ppermute | solution.py:552
  55.5 12.3 %collective-permute-start.9 = (bf16[4,1,144,384]{3,2,1,0:T(8,128)(2,1)S(1)}, bf16[4,1,144,384]{3,2,1,0:T(8,128)(2,1)S(1)}, u32[]{:S(2)}, u32[]{:S(2)}) collective-permute-start(bf16[4,1,144,384]{3,2,1,0:T(8,128)(2,1)S(1)} %get-tuple-element.67), channel_id=1, source_target_pairs={{0,2},{1,3},{2,0},{3,1},{4,6},{5,7},{6,4},{7,5},{8,10},{9,11},{10,... | collective-permute-start | bytes 1327112 | tf_op jit(solution)/shard_map/ppermute | solution.py:545
  59.4 14.2 %collective-permute-start.12 = (bf16[2,2,128,384]{3,2,1,0:T(8,128)(2,1)S(1)}, bf16[2,2,128,384]{3,2,1,0:T(8,128)(2,1)S(1)}, u32[]{:S(2)}, u32[]{:S(2)}) collective-permute-start(bf16[2,2,128,384]{3,2,1,0:T(8,128)(2,1)S(1)} %get-tuple-element.75), channel_id=1, source_target_pairs={{0,4},{1,5},{2,6},{3,7},{4,0},{5,1},{6,2},{7,3},{8,12},{9,13},{10,... | collective-permute-start | bytes 1179656 | tf_op jit(solution)/shard_map/ppermute | solution.py:545
  61.0 3.6 %collective-permute-start.5 = (f32[4,256]{1,0:T(4,128)S(1)}, f32[4,256]{1,0:T(4,128)S(1)}, u32[]{:S(2)}, u32[]{:S(2)}) collective-permute-start(f32[4,256]{1,0:T(4,128)S(1)} %get-tuple-element.59.done_ref), channel_id=1, source_target_pairs={{0,16},{16,0},{1,17},{17,1},{2,18},{18,2},{3,19},{19,3},{4,20},{20... | collective-permute-start | bytes 12296 | tf_op jit(solution)/shard_map/ppermute | solution.py:545
  67.9 15.9 %collective-permute-start.10 = (bf16[2,1,144,384]{3,2,0,1:T(8,128)(2,1)S(1)}, bf16[2,1,144,384]{3,2,0,1:T(8,128)(2,1)S(1)}, u32[]{:S(2)}, u32[]{:S(2)}) collective-permute-start(bf16[2,1,144,384]{3,2,0,1:T(8,128)(2,1)S(1)} %bitcast.43), channel_id=1, source_target_pairs={{0,4},{1,5},{2,6},{3,7},{4,0},{5,1},{6,2},{7,3},{8,12},{9,13},{10,... | collective-permute-start | bytes 663560 | tf_op jit(solution)/shard_map/ppermute | solution.py:545
  73.7 10.2 %collective-permute-start.13 = (bf16[1,2,128,384]{3,2,1,0:T(8,128)(2,1)S(1)}, bf16[1,2,128,384]{3,2,1,0:T(8,128)(2,1)S(1)}, u32[]{:S(2)}, u32[]{:S(2)}) collective-permute-start(bf16[1,2,128,384]{3,2,1,0:T(8,128)(2,1)S(1)} %get-tuple-element.77), channel_id=1, source_target_pairs={{0,8},{1,9},{2,10},{3,11},{4,12},{5,13},{6,14},{7,15},{8,0},{9,1},... | collective-permute-start | bytes 589832 | tf_op jit(solution)/shard_map/ppermute | solution.py:545
  83.8 7.1 %collective-permute-start.11 = (bf16[1,1,144,384]{3,2,1,0:T(8,128)(2,1)S(1)}, bf16[1,1,144,384]{3,2,1,0:T(8,128)(2,1)S(1)}, u32[]{:S(2)}, u32[]{:S(2)}) collective-permute-start(bf16[1,1,144,384]{3,2,1,0:T(8,128)(2,1)S(1)} %get-tuple-element.73), channel_id=1, source_target_pairs={{0,8},{1,9},{2,10},{3,11},{4,12},{5,13},{6,14},{7,15},{8,0},{9,1},... | collective-permute-start | bytes 331784 | tf_op jit(solution)/shard_map/ppermute | solution.py:545
  84.0 4.7 %collective-permute-start.14 = (bf16[1,1,128,384]{3,2,1,0:T(8,128)(2,1)S(1)}, bf16[1,1,128,384]{3,2,1,0:T(8,128)(2,1)S(1)}, u32[]{:S(2)}, u32[]{:S(2)}) collective-permute-start(bf16[1,1,128,384]{3,2,1,0:T(8,128)(2,1)S(1)} %get-tuple-element.79), channel_id=1, source_target_pairs={{0,2},{1,3},{2,0},{3,1},{4,6},{5,7},{6,4},{7,5},{8,10},{9,11},{10,... | collective-permute-start | bytes 294920 | tf_op jit(solution)/shard_map/ppermute | solution.py:545
